TPU v7x, 1024 devices: a whole 8x8x8 slice. The times are simulated.
1024 devices in a mesh: grp: 16 (over z, core), dev: 64 (over x, y).
Axes of the slice: x: 8, y: 8, z: 8, core: 2. Of those that a mesh axis runs over, the one named last changes fastest.
Arguments:
- offsets: float32 [3, 1048576], P(None, ('grp', 'dev')), may hold values from -0.5 to 0.5
- strengths: float32 [3, 1048576], P(None, ('grp', 'dev')), may hold values from -6 to 6
- cores: float32 [1048576], P(('grp', 'dev')), may hold values from 0.3 to 0.8
- place: int32 [2, 1048576], P(None, ('grp', 'dev')), may hold values from 0 to 16383, as said below
- near_list: int32 [14, 16384], P(None, ('grp', 'dev')), may hold values from -1 to 16383, as said below
- far_list: int32 [189, 16384], P(None, ('grp', 'dev')), may hold values from 0 to 16383, as said below
Outputs:
- velocity: float32 [3, 2097152], P(None, ('grp', 'dev'))
Inputs may be any that keep to these rules, and one draw needn't show every extreme that they name: `place`: row 0 names a cell of the particle's own group (cells of group g are g * 64 * 16 up to 64 * 16 more), row 1 a slot. Each pair of cell and slot is named at most once; a cell's slots are filled from 0 up without gaps, some cell of every device full; the cells of every device are named by exactly 1024 rows; at most 32 rows of one device name cells of one device, and every device has rows that reach that bound. `near_list`: used entries come first and are followed by -1; a cell's used entries differ and name cells of the same group held by the same device, the device before it or the device after it along dev. `far_list`: the entries of index under 189 // 2 name cells of the target cell's group.
All inputs are finite; a program needn't handle non-finite values.
Results may differ from a plain program's by a relative error of at most 0.0003.
Values sent between devices are 32-bit elements; how exact they have to be, the bound alone decides.
A program may use at most 64 MiB of HBM per device.

v0:
```python
import math

import jax
import jax.numpy as jnp
from jax import lax
from jax.sharding import PartitionSpec as P

SLOTS = 128


INV_FOUR_PI = 0.25 / math.pi


def extended(value, sides, width):
    for axis, dim in sides:
        size, length = (lax.axis_size(axis), value.shape[dim])
        up = [(i, (i + 1) % size) for i in range(size - 1)]
        down = [(j, i) for i, j in up]
        last = lax.slice_in_dim(value, length - width, length, axis=dim)
        first = lax.slice_in_dim(value, 0, width, axis=dim)
        before = lax.ppermute(last, axis, up)
        after = lax.ppermute(first, axis, down)
        value = jnp.concatenate([before, value, after], axis=dim)
    return value


def from_partner(value, axis, apart):
    mask = 2**apart
    pairs = [(source, source ^ mask) for source in range(lax.axis_size(axis))]
    return lax.ppermute(value, axis, pairs)


def centres(cell_ids):
    coordinate_list = []
    for axis_number in range(3):
        coordinate = jnp.zeros(cell_ids.shape, jnp.int32)
        for bit_level in range(10):
            power_shift = 3 * bit_level + axis_number
            coordinate = coordinate + cell_ids // (1 << power_shift) % 2 * (1 << bit_level)
        coordinate_list.append(coordinate.astype(jnp.float32) + 0.5)
    return jnp.stack(coordinate_list)


def near_terms(target, target_core, source, source_strength, source_core):
    delta_x = target[0][:, :, None] - source[0][:, None, :]
    delta_y = target[1][:, :, None] - source[1][:, None, :]
    delta_z = target[2][:, :, None] - source[2][:, None, :]
    spread = 0.5 * (target_core[:, :, None] ** 2 + source_core[:, None, :] ** 2)
    dist_sq = delta_x * delta_x + delta_y * delta_y + delta_z * delta_z + spread
    weight = INV_FOUR_PI / (dist_sq * jnp.sqrt(dist_sq))
    str_x = source_strength[0][:, None, :]
    str_y = source_strength[1][:, None, :]
    str_z = source_strength[2][:, None, :]
    vel_x = jnp.sum(weight * (str_y * delta_z - str_z * delta_y), axis=-1)
    vel_y = jnp.sum(weight * (str_z * delta_x - str_x * delta_z), axis=-1)
    vel_z = jnp.sum(weight * (str_x * delta_y - str_y * delta_x), axis=-1)
    return jnp.stack([vel_x, vel_y, vel_z])


def far_terms(target, target_core, centre_src, strength_src):
    delta_x = target[0][None] - centre_src[0][:, :, None]
    delta_y = target[1][None] - centre_src[1][:, :, None]
    delta_z = target[2][None] - centre_src[2][:, :, None]
    dist_sq = delta_x * delta_x + delta_y * delta_y + delta_z * delta_z + target_core[None] ** 2
    weight = INV_FOUR_PI / (dist_sq * jnp.sqrt(dist_sq))
    str_x = strength_src[0][:, :, None]
    str_y = strength_src[1][:, :, None]
    str_z = strength_src[2][:, :, None]
    vel_x = jnp.sum(weight * (str_y * delta_z - str_z * delta_y), axis=0)
    vel_y = jnp.sum(weight * (str_z * delta_x - str_x * delta_z), axis=0)
    vel_z = jnp.sum(weight * (str_x * delta_y - str_y * delta_x), axis=0)
    return jnp.stack([vel_x, vel_y, vel_z])


def pack_rows(dest_dev, spot_value, payload, dev_count, bucket_width):
    device_ids = jnp.arange(dev_count, dtype=jnp.int32)
    one_hot = (dest_dev[None, :] == device_ids[:, None]).astype(jnp.int32)
    running_rank = jnp.cumsum(one_hot, axis=1) - 1
    rank_row = jnp.sum(one_hot * running_rank, axis=0)
    target_slot = jnp.where(
        dest_dev < dev_count, dest_dev * bucket_width + rank_row, dev_count * bucket_width
    )
    packed = (
        jnp.zeros((payload.shape[0], dev_count * bucket_width), jnp.float32)
        .at[:, target_slot]
        .set(payload, mode="drop")
    )
    spot_ids = (
        jnp.full((1, dev_count * bucket_width), -1, jnp.int32)
        .at[0, target_slot]
        .set(spot_value, mode="drop")
    )
    return (packed, spot_ids)


def place_rows(received, received_spots, slot_total):
    slot_index = jnp.where(received_spots >= 0, received_spots, slot_total)
    slot_tile = (
        jnp.zeros((received.shape[0], slot_total), jnp.float32)
        .at[:, slot_index]
        .set(received, mode="drop")
    )
    filled = jnp.zeros((slot_total,), jnp.float32).at[slot_index].set(1.0, mode="drop")
    return (slot_tile, filled)


def per_device(offsets, strengths, cores, place, near_list, far_list):
    dev_count = lax.axis_size("dev")
    grp_count = lax.axis_size("grp")
    group_id = lax.axis_index("grp")
    device_id = lax.axis_index("dev")
    row_count = offsets.shape[1]
    cells_dev = near_list.shape[1]
    capacity = 2 * row_count // dev_count
    own_slots = cells_dev * SLOTS
    group_base = group_id * dev_count * cells_dev
    own_base = group_base + device_id * cells_dev
    payload = jnp.concatenate([offsets, strengths, cores[None, :]], axis=0)
    in_group = place[0] - group_base
    owner_dev = in_group // cells_dev
    spot_value = (in_group - owner_dev * cells_dev) * SLOTS + place[1]
    packed, spot_ids = pack_rows(owner_dev, spot_value, payload, dev_count, capacity)
    received, received_spots = (
        lax.all_to_all(packed, "dev", split_axis=1, concat_axis=1, tiled=True),
        lax.all_to_all(spot_ids, "dev", split_axis=1, concat_axis=1, tiled=True),
    )
    slot_tile, filled = place_rows(received, received_spots[0], own_slots)
    own_cells = own_base + jnp.arange(cells_dev, dtype=jnp.int32)
    own_pos = slot_tile[0:3].reshape(3, cells_dev, SLOTS) + centres(own_cells)[:, :, None]
    own_strength = slot_tile[3:6].reshape(3, cells_dev, SLOTS)
    own_core = jnp.where(filled > 0, slot_tile[6], 1.0)
    fill_own = filled.reshape(cells_dev, SLOTS)
    own_block = jnp.concatenate(
        [
            own_pos.reshape(3, own_slots),
            own_strength.reshape(3, own_slots),
            own_core.reshape(1, own_slots),
        ],
        axis=0,
    )
    wide_block = extended(own_block, (("dev", 1),), own_slots)
    ext_pos = wide_block[0:3].reshape(3, 3 * cells_dev, SLOTS)
    ext_strength = wide_block[3:6].reshape(3, 3 * cells_dev, SLOTS)
    ext_core = wide_block[6].reshape(3 * cells_dev, SLOTS)
    own_core_cells = ext_core[cells_dev : 2 * cells_dev]
    cell_strength = jnp.sum(own_strength, axis=2)
    strength_table = lax.all_gather(cell_strength, "dev", axis=1, tiled=True)
    for bit_number in range(grp_count.bit_length() - 1):
        partner = from_partner(strength_table, "grp", bit_number)
        upper_half = group_id // (1 << bit_number) % 2 == 1
        strength_table = jnp.where(
            upper_half,
            jnp.concatenate([partner, strength_table], axis=1),
            jnp.concatenate([strength_table, partner], axis=1),
        )
    far_count = far_list.shape[0]
    far_ids = far_list.reshape(far_count // 27, 27, cells_dev)
    far_centre = jnp.transpose(centres(far_ids), (1, 0, 2, 3))
    far_strength = jnp.transpose(strength_table[:, far_ids], (1, 0, 2, 3))
    entry_used = (near_list >= 0).astype(jnp.float32)
    local_ids = jnp.where(near_list >= 0, near_list - (own_base - cells_dev), 0)

    def evaluate(points_ext):
        target = points_ext[:, cells_dev : 2 * cells_dev]

        def near_step(running_sum, entry_pack):
            entry_ids, entry_weight = entry_pack
            term = near_terms(
                target,
                own_core_cells,
                points_ext[:, entry_ids],
                ext_strength[:, entry_ids],
                ext_core[entry_ids],
            )
            return (running_sum + entry_weight[None, :, None] * term, None)

        near_total, _ = lax.scan(
            near_step, jnp.zeros((3, cells_dev, SLOTS), jnp.float32), (local_ids, entry_used)
        )

        def far_step(running_sum, far_pack):
            centre_block, strength_block = far_pack
            return (
                running_sum + far_terms(target, own_core_cells, centre_block, strength_block),
                None,
            )

        far_total, _ = lax.scan(
            far_step, jnp.zeros((3, cells_dev, SLOTS), jnp.float32), (far_centre, far_strength)
        )
        return near_total + far_total

    first_pass = evaluate(ext_pos) * fill_own[None]
    moved_own = own_pos + 0.25 * first_pass
    moved_ext = extended(moved_own.reshape(3, own_slots), (("dev", 1),), own_slots).reshape(
        3, 3 * cells_dev, SLOTS
    )
    second_pass = evaluate(moved_ext) * fill_own[None]
    return (0.5 * (first_pass + second_pass)).reshape(3, own_slots)


def solution(mesh):
    placed = (
        P(None, ("grp", "dev")),
        P(None, ("grp", "dev")),
        P(("grp", "dev")),
        P(None, ("grp", "dev")),
        P(None, ("grp", "dev")),
        P(None, ("grp", "dev")),
    )
    return jax.shard_map(
        per_device, mesh=mesh, in_specs=placed, out_specs=P(None, ("grp", "dev")), check_vma=False
    )
```

profile of v0, /device:TPU:8, one launch (start us, length us, event | category | flops | bytes accessed | tf_op | source)
XLA Modules:
  0.0 398.4 jit_solution(9300492916975661405)
XLA Ops:
  0.8 18.0 %reduce-window.6 = s32[64,8,128]{2,1,0:T(8,128)S(1)} reduce-window(s32[64,8,128]{2,1,0:T(8,128)S(1)} %fusion.60, s32[]{:T(128)} %constant.1015.clone.1), window={size=1x1x128 pad=0_0x0_0x127_0}, to_apply=%region_0.1 | reduce-window | flops 8323072 | bytes 524292 | tf_op jit(solution)/shard_map/reduce-window
  20.9 4.3 %scatter_custom_fusion.3 = s32[2048]{0:T(1024)S(1)} fusion(s32[1024]{0:T(1024)S(1)} %get-tuple-element.734, s32[1024]{0:T(1024)S(1)} %get-tuple-element.733, s32[]{:T(128)} %constant.1023.clone.1), kind=kCustom, calls=%fused_computation.528 | custom fusion | bytes 8196
  26.0 17.3 %all-to-all-start = ((s32[1,64,32]{2,0,1:T(1,128)}), s32[1,64,32]{2,0,1:T(1,128)S(1)}, u32[]{:S(2)}, u32[]{:S(2)}) async-start(s32[1,64,32]{2,0,1:T(1,128)} %bitcast.6), calls=%async_computation | async-start | bytes 65536 | tf_op jit(solution)/shard_map/all_to_all | solution.py:125
  45.1 1.3 fusion.217
  46.3 1.3 subtract_select_fusion
  47.6 1.6 fusion.71
  51.3 3.3 scatter_custom_fusion
  56.2 12.7 %all-to-all-start.1 = ((f32[64,1,224]{2,1,0:T(1,128)}), f32[64,1,224]{2,1,0:T(1,128)S(1)}, u32[]{:S(2)}, u32[]{:S(2)}) async-start(f32[64,1,224]{2,1,0:T(1,128)} %reshape.4666), calls=%async_computation.1 | async-start | bytes 131072 | tf_op jit(solution)/shard_map/all_to_all | solution.py:124
  70.2 8.6 %scatter_custom_fusion.2 = f32[2048]{0:T(1024)} fusion(s32[2048]{0:T(1024)S(1)} %bitcast.323, f32[2048]{0:T(1024)S(1)} %broadcast.5237, f32[]{:T(128)} %constant.1016.clone.1), kind=kCustom, calls=%fused_computation.530 | custom fusion | bytes 8196 | tf_op jit(solution)/shard_map/scatter | solution.py:103
  80.9 6.0 %scatter_custom_fusion.1 = f32[7,2048]{0,1:T(8,128)S(1)} fusion(s32[2048]{0:T(1024)S(1)} %bitcast.324, f32[2048,7]{1,0:T(8,128)S(1)} %copy.129, f32[]{:T(128)} %constant.1016.clone.1), kind=kCustom, calls=%fused_computation.145 | custom fusion | bytes 57348 | tf_op jit(solution)/shard_map/scatter | solution.py:101
  86.9 1.2 slice_reduce_fusion
  88.1 0.9 bitcast_reduce_fusion
  89.1 2.1 bitcast_add_fusion
  91.2 1.6 copy.132
  93.8 48.4 %all-gather = f32[64,16,3]{1,2,0:T(4,128)S(1)} all-gather(f32[1,16,3]{1,2,0:T(4,128)S(1)} %bitcast.320), channel_id=1, replica_groups=mesh['grp'=16,'dev'=64] {'dev'}, dimensions={0}, use_global_device_ids=true | all-gather | bytes 12480 | tf_op jit(solution)/shard_map/all_gather | solution.py:147
  142.3 1.9 collective-permute-start.2
  145.0 4.6 %collective-permute-start.1 = (f32[7,2048]{1,0:T(8,128)S(1)}, f32[7,2048]{1,0:T(8,128)S(1)}, u32[]{:S(2)}, u32[]{:S(2)}) collective-permute-start(f32[7,2048]{1,0:T(8,128)S(1)} %pad_maximum_fusion.4), channel_id=1, source_target_pairs={{1,0},{2,1},{3,2},{4,3},{5,4},{6,5},{7,6},{8,7},{9,8},{10,9},{11,1... | collective-permute-start | bytes 172040 | tf_op jit(solution)/shard_map/ppermute | solution.py:22
  149.6 1.9 collective-permute-start
  151.6 1.9 collective-permute-start.3
  153.5 0.9 copy.142
  154.4 2.9 collective-permute-done.3
  157.4 5.4 %collective-permute-start.4 = (f32[3,4096]{1,0:T(4,128)S(1)}, f32[3,4096]{1,0:T(4,128)S(1)}, u32[]{:S(2)}, u32[]{:S(2)}) collective-permute-start(f32[3,4096]{1,0:T(4,128)S(1)} %maximum_select_fusion.1), channel_id=1, source_target_pairs={{0,256},{64,320},{128,384},{192,448},{256,0},{320,64},{384,128},{4... | collective-permute-start | bytes 147464 | tf_op jit(solution)/shard_map/ppermute | solution.py:30
  163.0 2.6 collective-permute-done.4
  165.6 11.9 %collective-permute-start.5 = (f32[3,8192]{1,0:T(4,128)S(1)}, f32[3,8192]{1,0:T(4,128)S(1)}, u32[]{:S(2)}, u32[]{:S(2)}) collective-permute-start(f32[3,8192]{1,0:T(4,128)S(1)} %maximum_select_fusion), channel_id=1, source_target_pairs={{0,512},{64,576},{128,640},{192,704},{256,768},{320,832},{384,896}... | collective-permute-start | bytes 294920 | tf_op jit(solution)/shard_map/ppermute | solution.py:30
  177.5 85.3 %while.52 = (s32[]{:T(128)}, f32[3,16,128]{2,1,0:T(8,128)S(1)}, f32[14,16]{1,0:T(8,128)}, f32[3,16,128]{2,1,0:T(8,128)S(1)}, s32[14,16]{1,0:T(8,128)}, /*index=5...) while((s32[]{:T(128)}, f32[3,16,128]{2,1,0:T(8,128)S(1)}, ...), condition=%wide.region_11.12_spmd.clone, body=%wide.region_7.11_spmd.clone.sunk | while | flops 7367731 | bytes 479943 | solution.py:177
  180.0 2.8 fusion.322
  186.1 2.8 fusion.322
  192.2 2.8 fusion.322
  198.3 2.8 fusion.322
  204.4 2.8 fusion.322
  210.4 2.8 fusion.322
  216.5 2.8 fusion.322
  222.6 2.8 fusion.322
  228.7 2.8 fusion.322
  234.8 2.8 fusion.322
  240.9 2.8 fusion.322
  247.0 2.8 fusion.322
  253.1 2.8 fusion.322
  259.2 2.8 fusion.322
  263.5 5.1 %copy.137 = f32[3,16384]{0,1:T(8,128)} copy(f32[3,16384]{1,0:T(4,128)S(1)} %get-tuple-element.725) | data formatting | bytes 393216 | tf_op jit(solution)/shard_map/concatenate | solution.py:153
  268.6 5.0 %copy.138 = f32[3,16384]{0,1:T(8,128)} copy(f32[3,16384]{1,0:T(4,128)S(1)} %get-tuple-element.724) | data formatting | bytes 393216 | tf_op jit(solution)/shard_map/concatenate | solution.py:154
  273.6 5.9 %broadcast_select_fusion = f32[3,16384]{0,1:T(8,128)} fusion(f32[3,16384]{0,1:T(8,128)} %copy.137, f32[3,16384]{0,1:T(8,128)} %copy.138, pred[]{:T(512)S(6)} %eq.100), kind=kLoop, calls=%fused_computation.141 | loop fusion | flops 49152 | bytes 589825 | tf_op jit(solution)/shard_map/jit(_where)/select_n | solution.py:151
  279.5 11.6 %gather_fusion.6 = f32[3024,3]{1,0:T(8,128)S(1)} fusion(f32[3,16384]{0,1:T(8,128)} %broadcast_select_fusion, s32[3072]{0:T(1024)S(1)} %pad_clamp_fusion.2), kind=kCustom, calls=%fused_computation.6 | custom fusion | bytes 84672 | tf_op jit(solution)/shard_map/gather | solution.py:159
  291.2 1.5 copy.140
  292.7 3.4 while.53
  296.3 7.0 %collective-permute-start.7 = (f32[3,2048]{1,0:T(4,128)S(1)}, f32[3,2048]{1,0:T(4,128)S(1)}, u32[]{:S(2)}, u32[]{:S(2)}) collective-permute-start(f32[3,2048]{1,0:T(4,128)S(1)} %bitcast.313), channel_id=1, source_target_pairs={{1,0},{2,1},{3,2},{4,3},{5,4},{6,5},{7,6},{8,7},{9,8},{10,9},{11,1... | collective-permute-start | bytes 73736 | tf_op jit(solution)/shard_map/ppermute | solution.py:22
  303.2 1.9 collective-permute-start.6
  305.2 3.4 while.55
  308.7 3.7 collective-permute-done.6
  312.5 85.3 %while.54 = (s32[]{:T(128)}, f32[3,16,128]{2,1,0:T(8,128)S(1)}, f32[14,16]{1,0:T(8,128)}, f32[3,16,128]{2,1,0:T(8,128)S(1)}, s32[14,16]{1,0:T(8,128)}, /*index=5...) while((s32[]{:T(128)}, f32[3,16,128]{2,1,0:T(8,128)S(1)}, ...), condition=%wide.region_22.23_spmd.clone, body=%wide.region_18.22_spmd.clone.sunk | while | flops 7367731 | bytes 479943 | solution.py:177
  315.0 2.8 fusion.328
  321.1 2.8 fusion.328
  327.2 2.8 fusion.328
  333.2 2.8 fusion.328
  339.3 2.8 fusion.328
  345.4 2.8 fusion.328
  351.5 2.8 fusion.328
  357.6 2.8 fusion.328
  363.7 2.8 fusion.328
  369.8 2.8 fusion.328
  375.9 2.8 fusion.328
  382.0 2.8 fusion.328
  388.1 2.8 fusion.328
  394.2 2.8 fusion.328
  (451 shorter events, 112.6 us)
Async XLA Ops:
  26.0 30.2 %all-to-all-start = ((s32[1,64,32]{2,0,1:T(1,128)}), s32[1,64,32]{2,0,1:T(1,128)S(1)}, u32[]{:S(2)}, u32[]{:S(2)}) async-start(s32[1,64,32]{2,0,1:T(1,128)} %bitcast.6), calls=%async_computation | async-start | bytes 65536 | tf_op jit(solution)/shard_map/all_to_all | solution.py:125
  56.2 22.7 %all-to-all-start.1 = ((f32[64,1,224]{2,1,0:T(1,128)}), f32[64,1,224]{2,1,0:T(1,128)S(1)}, u32[]{:S(2)}, u32[]{:S(2)}) async-start(f32[64,1,224]{2,1,0:T(1,128)} %reshape.4666), calls=%async_computation.1 | async-start | bytes 131072 | tf_op jit(solution)/shard_map/all_to_all | solution.py:124
  142.3 9.2 %collective-permute-start.2 = (f32[3,1024]{1,0:T(4,128)S(1)}, f32[3,1024]{1,0:T(4,128)S(1)}, u32[]{:S(2)}, u32[]{:S(2)}) collective-permute-start(f32[3,1024]{1,0:T(4,128)S(1)} %bitcast.306), channel_id=1, source_target_pairs={{0,64},{64,0},{128,192},{192,128},{256,320},{320,256},{384,448},{4... | collective-permute-start | bytes 36872 | tf_op jit(solution)/shard_map/ppermute | solution.py:30
  145.0 17.8 %collective-permute-start.1 = (f32[7,2048]{1,0:T(8,128)S(1)}, f32[7,2048]{1,0:T(8,128)S(1)}, u32[]{:S(2)}, u32[]{:S(2)}) collective-permute-start(f32[7,2048]{1,0:T(8,128)S(1)} %pad_maximum_fusion.4), channel_id=1, source_target_pairs={{1,0},{2,1},{3,2},{4,3},{5,4},{6,5},{7,6},{8,7},{9,8},{10,9},{11,1... | collective-permute-start | bytes 172040 | tf_op jit(solution)/shard_map/ppermute | solution.py:22
  149.6 13.2 %collective-permute-start = (f32[7,2048]{1,0:T(8,128)S(1)}, f32[7,2048]{1,0:T(8,128)S(1)}, u32[]{:S(2)}, u32[]{:S(2)}) collective-permute-start(f32[7,2048]{1,0:T(8,128)S(1)} %pad_maximum_fusion.4), channel_id=1, source_target_pairs={{0,1},{1,2},{2,3},{3,4},{4,5},{5,6},{6,7},{7,8},{8,9},{9,10},{10,1... | collective-permute-start | bytes 172040 | tf_op jit(solution)/shard_map/ppermute | solution.py:21
  151.6 5.8 %collective-permute-start.3 = (f32[3,2048]{1,0:T(4,128)S(1)}, f32[3,2048]{1,0:T(4,128)S(1)}, u32[]{:S(2)}, u32[]{:S(2)}) collective-permute-start(f32[3,2048]{1,0:T(4,128)S(1)} %maximum_select_fusion.2), channel_id=1, source_target_pairs={{0,128},{64,192},{128,0},{192,64},{256,384},{320,448},{384,256},{4... | collective-permute-start | bytes 73736 | tf_op jit(solution)/shard_map/ppermute | solution.py:30
  157.4 8.2 %collective-permute-start.4 = (f32[3,4096]{1,0:T(4,128)S(1)}, f32[3,4096]{1,0:T(4,128)S(1)}, u32[]{:S(2)}, u32[]{:S(2)}) collective-permute-start(f32[3,4096]{1,0:T(4,128)S(1)} %maximum_select_fusion.1), channel_id=1, source_target_pairs={{0,256},{64,320},{128,384},{192,448},{256,0},{320,64},{384,128},{4... | collective-permute-start | bytes 147464 | tf_op jit(solution)/shard_map/ppermute | solution.py:30
  165.6 97.8 %collective-permute-start.5 = (f32[3,8192]{1,0:T(4,128)S(1)}, f32[3,8192]{1,0:T(4,128)S(1)}, u32[]{:S(2)}, u32[]{:S(2)}) collective-permute-start(f32[3,8192]{1,0:T(4,128)S(1)} %maximum_select_fusion), channel_id=1, source_target_pairs={{0,512},{64,576},{128,640},{192,704},{256,768},{320,832},{384,896}... | collective-permute-start | bytes 294920 | tf_op jit(solution)/shard_map/ppermute | solution.py:30
  262.8 0.6 copy-start.4
  273.6 22.5 %copy-start.2 = (f32[2048]{0:T(1024)S(1)}, f32[2048]{0:T(1024)}, u32[]{:S(2)}) copy-start(f32[2048]{0:T(1024)} %scatter_custom_fusion.2) | copy-start | bytes 24580
  273.6 22.5 %copy-start.3 = (f32[3,16,128]{2,1,0:T(8,128)S(1)}, f32[3,16,128]{2,1,0:T(8,128)}, u32[]{:S(2)}) copy-start(f32[3,16,128]{2,1,0:T(8,128)} %copy.142) | copy-start | bytes 73732
  273.6 31.5 %copy-start.1 = (f32[3,16,128]{2,1,0:T(8,128)S(1)}, f32[3,16,128]{2,1,0:T(8,128)}, u32[]{:S(2)}) copy-start(f32[3,16,128]{2,1,0:T(8,128)} %custom-call.3) | copy-start | bytes 73732
  279.5 32.9 %copy-start = (f32[3,16,128]{2,1,0:T(8,128)S(1)}, f32[3,16,128]{2,1,0:T(8,128)}, u32[]{:S(2)}) copy-start(f32[3,16,128]{2,1,0:T(8,128)} %custom-call.2) | copy-start | bytes 73732
  279.5 32.9 %copy-start.5 = (f32[16,128,1]{1,0,2:T(8,128)S(1)}, f32[16,128,1]{1,0,2:T(8,128)}, u32[]{:S(2)}) copy-start(f32[16,128,1]{1,0,2:T(8,128)} %copy-done.4) | copy-start | bytes 24580
  296.3 12.4 %collective-permute-start.7 = (f32[3,2048]{1,0:T(4,128)S(1)}, f32[3,2048]{1,0:T(4,128)S(1)}, u32[]{:S(2)}, u32[]{:S(2)}) collective-permute-start(f32[3,2048]{1,0:T(4,128)S(1)} %bitcast.313), channel_id=1, source_target_pairs={{1,0},{2,1},{3,2},{4,3},{5,4},{6,5},{7,6},{8,7},{9,8},{10,9},{11,1... | collective-permute-start | bytes 73736 | tf_op jit(solution)/shard_map/ppermute | solution.py:22
  303.2 9.1 %collective-permute-start.6 = (f32[3,2048]{1,0:T(4,128)S(1)}, f32[3,2048]{1,0:T(4,128)S(1)}, u32[]{:S(2)}, u32[]{:S(2)}) collective-permute-start(f32[3,2048]{1,0:T(4,128)S(1)} %bitcast.314), channel_id=1, source_target_pairs={{0,1},{1,2},{2,3},{3,4},{4,5},{5,6},{6,7},{7,8},{8,9},{9,10},{10,1... | collective-permute-start | bytes 73736 | tf_op jit(solution)/shard_map/ppermute | solution.py:21
where the time goes:
time: 402 us; the launch traced here: 398 us
  other arithmetic  143 us (36%)
  local copies, waits for them, and re-layouts  128 us (32%)
  starting transfers between devices  66.6 us (17%)
  blocking collectives  48.4 us (12%)
  waiting for transfers between devices  9.22 us (2%)
    reduce_sum x28, other arithmetic, near_terms(): vel_x = jnp.sum(weight * (str_y * delta_z - str_z * delta_y), axis=-1)  78.8 us
    all_gather x1, blocking collectives, per_device(): strength_table = lax.all_gather(cell_strength, 'dev', axis=1, tiled=True)  48.4 us
    ppermute x4, starting transfers between devices, from_partner(): return lax.ppermute(value, axis, pairs)  21.1 us
    mul x28, local copies, waits for them, and re-layouts, near_step(): return (running_sum + entry_weight[None, :, None] * term, None)  19.4 us
    select_n x28, other arithmetic, near_step(): points_ext[:, entry_ids]  19 us
    another operation x2, other arithmetic  18 us
    all_to_all x1, starting transfers between devices, per_device(): lax.all_to_all(spot_ids, 'dev', split_axis=1, concat_axis=1, tiled=True)  17.3 us
    gather x28, local copies, waits for them, and re-layouts, near_step(): points_ext[:, entry_ids]  16.4 us
  transfers between devices with their start and end apart: 10, of which 3 were waited for; matrix products, arithmetic and copies ran while one was open for 28% of the time, Pallas kernels for 0%

commit v1 on v0

v1 whole, which is shorter than its diff:
```python
import functools
import math

import jax
import jax.numpy as jnp
from jax import lax
from jax.experimental import pallas as pl
from jax.experimental.pallas import tpu as pltpu
from jax.sharding import PartitionSpec as P

SLOTS = 128
CELLS = 16
CAP = 32
NEAR = 14
FAR = 189
N = 8
INV_FOUR_PI = 0.25 / math.pi
MESH = pl.DeviceIdType.MESH
F32 = jnp.float32
BF16 = jnp.bfloat16

NEAR_CHUNKS = 3 * CELLS
DUMMY = NEAR_CHUNKS
FAR_BASE = NEAR_CHUNKS + 2
CHUNKS = FAR_BASE + 2 * CELLS
FEATS = 48


def nt(a, b):
    return lax.dot_general(a, b, (((1,), (1,)), ((), ())), preferred_element_type=F32)


def nn(a, b):
    return lax.dot_general(a, b, (((1,), (0,)), ((), ())), preferred_element_type=F32)


def rows_of(shape):
    return lax.broadcasted_iota(jnp.int32, shape, len(shape) - 2)


def lanes_of(shape):
    return lax.broadcasted_iota(jnp.int32, shape, len(shape) - 1)


def split2(value):
    high = value.astype(BF16).astype(F32)
    return jnp.concatenate([high, value - high], axis=0)


def route_kernel(
    off_ref, str_ref, core_ref, place_ref, ext_ref, table_ref,
    fields, spread, send1, recv1, send2, recv2, sums, sums_y, sums_x,
    sx_s, sx_r, sy_s, sy_r, halo_s, halo_r, cy_s, cy_r, cx_s, cx_r, cz_s, cz_r, cc_s, cc_r,
):
    dev = lax.axis_index("dev")
    grp = lax.axis_index("grp")
    x, y = dev // N, dev % N
    z, core = grp // 2, grp % 2

    def x_peer(k):
        return (x + k) % N

    def y_peer(k):
        return (y + k) % N

    def z_peer(k):
        return (z + k) % N

    right, left = (dev + 1) % (N * N), (dev + N * N - 1) % (N * N)
    barrier = pltpu.get_barrier_semaphore()
    for k in range(1, N):
        pl.semaphore_signal(barrier, 1, device_id={"dev": x_peer(k) * N + y}, device_id_type=MESH)
        pl.semaphore_signal(barrier, 1, device_id={"dev": x * N + y_peer(k)}, device_id_type=MESH)
        pl.semaphore_signal(barrier, 1, device_id={"grp": z_peer(k) * 2 + core}, device_id_type=MESH)
    pl.semaphore_signal(barrier, 1, device_id={"dev": right}, device_id_type=MESH)
    pl.semaphore_signal(barrier, 1, device_id={"dev": left}, device_id_type=MESH)
    pl.semaphore_signal(barrier, 1, device_id={"grp": z * 2 + (1 - core)}, device_id_type=MESH)

    rows = off_ref.shape[1]
    cell_row = place_ref[0:1, :]
    spot = (cell_row & (CELLS - 1)) * SLOTS + place_ref[1:2, :] + 1
    owner = (cell_row >> 4) & (N * N - 1)
    fields[0:3, :] = off_ref[...]
    fields[3:4, :] = core_ref[...]
    fields[4:5, :] = spot.astype(F32)
    fields[5:8, :] = str_ref[...]
    both = split2(fields[...])
    earlier = rows_of((SLOTS, 2 * SLOTS)) < lanes_of((SLOTS, 2 * SLOTS))
    counter = jnp.where(earlier | (lanes_of((SLOTS, 2 * SLOTS)) >= SLOTS), 1.0, 0.0).astype(BF16)
    carry = jnp.zeros((N * N, SLOTS), F32)
    ranks = []
    for b in range(rows // SLOTS):
        hot = jnp.where(rows_of((N * N, SLOTS)) == owner[:, b * SLOTS : (b + 1) * SLOTS], 1.0, 0.0)
        count = nn(hot.astype(BF16), counter)
        ranks.append(jnp.sum(hot * (count[:, :SLOTS] + carry), axis=0, keepdims=True))
        carry = carry + count[:, SLOTS:]
    rank = jnp.concatenate(ranks, axis=1).astype(jnp.int32)
    low = (owner & 3) * CAP + rank
    high = owner >> 2
    low_hot = jnp.where(rows_of((SLOTS, rows)) == low, 1.0, 0.0).astype(BF16)
    for t in range(2 * N):
        spread[16 * t : 16 * t + 16, 0:rows] = jnp.where(high == t, both, 0.0).astype(BF16)
    packed = nt(spread[:, 0:rows], low_hot)
    for t in range(2 * N):
        send1[t] = packed[16 * t : 16 * t + 8] + packed[16 * t + 8 : 16 * t + 16]

    pl.semaphore_wait(barrier, 3 * (N - 1) + 3)

    copies = []
    for k in range(1, N):
        to = x_peer(k)
        copy = pltpu.make_async_remote_copy(
            src_ref=send1.at[pl.ds(2 * to, 2)], dst_ref=recv1.at[x],
            send_sem=sx_s.at[k], recv_sem=sx_r.at[k],
            device_id={"dev": to * N + y}, device_id_type=MESH,
        )
        copy.start()
        copies.append(copy)
    recv1[x] = send1[pl.ds(2 * x, 2)]
    for copy in copies:
        copy.wait_recv()
    lane_group = lanes_of((8, SLOTS)) // CAP
    for t in range(N):
        for k in range(2):
            tile = None
            for g in range(4):
                part = recv1[4 * k + g, t // 4]
                turn = (g - t % 4) % 4 * CAP
                if turn:
                    part = pltpu.roll(part, turn, 1)
                tile = part if tile is None else jnp.where(lane_group == g, part, tile)
            send2[t, k] = tile
    for k in range(1, N):
        to = y_peer(k)
        copy = pltpu.make_async_remote_copy(
            src_ref=send2.at[to], dst_ref=recv2.at[y],
            send_sem=sy_s.at[k], recv_sem=sy_r.at[k],
            device_id={"dev": x * N + to}, device_id_type=MESH,
        )
        copy.start()
        copies.append(copy)
    recv2[y] = send2[y]
    for copy in copies[N - 1 :]:
        copy.wait_recv()

    slot_rows, sums_rows, both_all = [], [], []
    for t in range(2 * N):
        tile = recv2[t // 2, t % 2]
        spot_row = tile[4:5, :] - 1.0
        cell = jnp.floor(spot_row * (1.0 / SLOTS))
        slot = (spot_row - cell * SLOTS).astype(jnp.int32)
        cell = cell.astype(jnp.int32)
        two = split2(tile)
        both_all.append(two.astype(BF16))
        slot_rows.append(jnp.where(rows_of((SLOTS, SLOTS)) == slot, 1.0, 0.0).astype(BF16))
        sums_rows.append(
            jnp.where(rows_of((SLOTS, SLOTS)) == cell + y * CELLS, 1.0, 0.0).astype(BF16)
        )
        for c in range(CELLS):
            spread[16 * c : 16 * c + 16, t * SLOTS : (t + 1) * SLOTS] = jnp.where(
                cell == c, two, 0.0
            ).astype(BF16)
    cell_sums = nt(jnp.concatenate(both_all, axis=1), jnp.concatenate(sums_rows, axis=1))
    sums[...] = cell_sums[0:8] + cell_sums[8:16]
    sum_copies = []
    for k in range(1, N):
        copy = pltpu.make_async_remote_copy(
            src_ref=sums, dst_ref=sums_y.at[y],
            send_sem=cy_s.at[k], recv_sem=cy_r.at[k],
            device_id={"dev": x * N + y_peer(k)}, device_id_type=MESH,
        )
        copy.start()
        sum_copies.append(copy)
    placed = nt(spread[...], jnp.concatenate(slot_rows, axis=1))
    for c in range(CELLS):
        tile = placed[16 * c : 16 * c + 8] + placed[16 * c + 8 : 16 * c + 16]
        empty = (rows_of((8, SLOTS)) == 3) & (tile[4:5, :] == 0.0)
        ext_ref[CELLS + c] = jnp.where(empty, 1.0, tile)

    halo = []
    for i, (to, at) in enumerate(((right, 0), (left, 2 * CELLS))):
        copy = pltpu.make_async_remote_copy(
            src_ref=ext_ref.at[pl.ds(CELLS, CELLS)], dst_ref=ext_ref.at[pl.ds(at, CELLS)],
            send_sem=halo_s.at[i], recv_sem=halo_r.at[i],
            device_id={"dev": to}, device_id_type=MESH,
        )
        copy.start()
        halo.append(copy)

    total = sums[...]
    for copy in sum_copies:
        copy.wait_recv()
    for k in range(1, N):
        total = total + sums_y[y_peer(k)]
    sums_x[x] = total
    x_copies = []
    for k in range(1, N):
        copy = pltpu.make_async_remote_copy(
            src_ref=sums_x.at[x], dst_ref=sums_x.at[x],
            send_sem=cx_s.at[k], recv_sem=cx_r.at[k],
            device_id={"dev": x_peer(k) * N + y}, device_id_type=MESH,
        )
        copy.start()
        x_copies.append(copy)
    for copy in x_copies:
        copy.wait_recv()
    for comp in range(3):
        table_ref[core, z, comp] = sums_x[:, 5 + comp, :]
    z_copies = []
    for k in range(1, N):
        copy = pltpu.make_async_remote_copy(
            src_ref=table_ref.at[core, z], dst_ref=table_ref.at[core, z],
            send_sem=cz_s.at[k], recv_sem=cz_r.at[k],
            device_id={"grp": z_peer(k) * 2 + core}, device_id_type=MESH,
        )
        copy.start()
        z_copies.append(copy)
    core_copies = []
    for k in range(N):
        if k:
            z_copies[k - 1].wait_recv()
        source = (z + N - k) % N
        copy = pltpu.make_async_remote_copy(
            src_ref=table_ref.at[core, source], dst_ref=table_ref.at[core, source],
            send_sem=cc_s.at[k], recv_sem=cc_r.at[k],
            device_id={"grp": z * 2 + (1 - core)}, device_id_type=MESH,
        )
        copy.start()
        core_copies.append(copy)
    for copy in core_copies + halo:
        copy.wait_recv()
    for copy in copies + sum_copies + x_copies + z_copies + core_copies + halo:
        copy.wait_send()


def halo_kernel(moved_ref, ext_ref, send_sem, recv_sem):
    dev = lax.axis_index("dev")
    right, left = (dev + 1) % (N * N), (dev + N * N - 1) % (N * N)
    barrier = pltpu.get_barrier_semaphore()
    for to in (right, left):
        pl.semaphore_signal(barrier, 1, device_id={"dev": to}, device_id_type=MESH)
    pl.semaphore_wait(barrier, 2)
    halo = []
    for i, to in enumerate((right, left)):
        copy = pltpu.make_async_remote_copy(
            src_ref=moved_ref, dst_ref=ext_ref.at[i],
            send_sem=send_sem.at[i], recv_sem=recv_sem.at[i],
            device_id={"dev": to}, device_id_type=MESH,
        )
        copy.start()
        halo.append(copy)
    for copy in halo:
        copy.wait()


def axis_bits(ids):
    shifted = ids >> jnp.minimum(rows_of(ids.shape), 2)
    value = shifted & 1
    for bit in range(1, 5):
        value = value + ((shifted >> (3 * bit)) & 1) * (1 << bit)
    return value


def source_rows(points, half, flag):
    row = rows_of(points.shape)
    at = jnp.where(row < 3, points, 0.0)
    norm = jnp.sum(at * at, axis=0, keepdims=True) + half
    return jnp.where(row == 3, norm, jnp.where(row == 4, 1.0, jnp.where(row == 5, flag, at)))


def split3(tile):
    high = tile.astype(BF16).astype(F32)
    rest = tile - high
    mid = rest.astype(BF16).astype(F32)
    return high, mid, rest - mid


def moments(points, strength):
    sx, sy, sz = (INV_FOUR_PI * s for s in strength)
    px, py, pz = points
    row = rows_of((8, sx.shape[1]))
    tile = jnp.zeros((8, sx.shape[1]), F32)
    values = (sx, sy, sz, sy * pz - sz * py, sz * px - sx * pz, sx * py - sy * px)
    for r, value in enumerate(values):
        tile = jnp.where(row == r, value, tile)
    return split2(tile).astype(BF16)


def pass_kernel(
    second, near_ref, own_ref, ext_ref, *rest
):
    if second:
        move_ref, moved_ref, first_ref, far_in, out_ref, feat, weight, targ, count, acc = rest
    else:
        table_ref, far_ref, first_ref, moved_ref, far_out, feat, weight, targ, count, acc = rest
    base_id = own_ref[0]
    base = axis_bits(jnp.full((8, SLOTS), base_id, jnp.int32))

    def put(chunk, tile, points):
        high, mid, low = split3(tile)
        feat[chunk] = jnp.concatenate([high, high, mid, mid, high, low], axis=0).astype(BF16)

    def own_tile(l):
        tile = ext_ref[l]
        ids = jnp.full((8, SLOTS), base_id - CELLS + l, jnp.int32)
        centre = (axis_bits(ids) - base).astype(F32)
        return tile, centre

    def near_prep(l, _):
        tile, centre = own_tile(l)
        at = tile
        if second:
            side = l // CELLS
            within = l - side * CELLS
            at = jnp.where(
                side == 1, moved_ref[within],
                jnp.where(side == 0, move_ref[0, within], move_ref[1, within]),
            )
        points = at + centre
        core = tile[3:4, :]
        half = 0.5 * core * core
        put(l, source_rows(points, half, 0.0), points)
        weight[l] = moments(
            (points[0:1], points[1:2], points[2:3]), (tile[5:6], tile[6:7], tile[7:8])
        )
        return 0

    lax.fori_loop(0, NEAR_CHUNKS, near_prep, 0)
    feat[DUMMY] = jnp.zeros((FEATS, SLOTS), BF16)
    weight[DUMMY] = jnp.zeros((16, SLOTS), BF16)

    def target_prep(c, _):
        tile, centre = own_tile(CELLS + c)
        at = moved_ref[c] if second else tile
        points = at + centre
        row = rows_of(points.shape)
        core = tile[3:4, :]
        half = 0.5 * core * core
        pos = jnp.where(row < 3, points, 0.0)
        norm = jnp.sum(pos * pos, axis=0, keepdims=True) + half
        value = jnp.where(
            row == 3, 1.0, jnp.where(row == 4, norm, jnp.where(row == 5, half, -2.0 * pos))
        )
        high, mid, low = split3(value)
        stack = jnp.concatenate([high, mid, high, mid, low, high], axis=0)
        stack = jnp.concatenate([stack, jnp.zeros((SLOTS - FEATS, SLOTS), F32)], axis=0)
        targ[c] = stack.T.astype(BF16)
        return 0

    lax.fori_loop(0, CELLS, target_prep, 0)

    if not second:
        far_pad = jnp.concatenate(
            [far_ref[...].astype(F32), jnp.full((3, CELLS), -1.0, F32)], axis=0
        )
        far_pad = jnp.concatenate([far_pad, jnp.full((256 - 192, CELLS), -1.0, F32)], axis=0)
        far_pad = jnp.concatenate([far_pad, jnp.full((256, SLOTS - CELLS), -1.0, F32)], axis=1)
        acc[...] = jnp.concatenate([far_pad[0:128].T, far_pad[128:256].T], axis=1)[0:CELLS]
        table = table_ref[...].reshape(2 * N * 3 * N, SLOTS)
        table_high = table.astype(BF16)
        table_low = (table - table_high.astype(F32)).astype(BF16)
        table2 = jnp.concatenate([table_high, table_low], axis=1)

        def far_gather(c, _):
            ids = acc[pl.ds(c, 1), :].astype(jnp.int32)
            lane_hot = jnp.where(rows_of((SLOTS, 256)) == (ids & 127), 1.0, 0.0).astype(BF16)
            got = nn(table2, jnp.concatenate([lane_hot, lane_hot], axis=0))
            high = ids >> 7
            sums = [jnp.zeros((8, 256), F32) for _ in range(3)]
            for g in range(2 * N):
                start = (g % 2) * N * 3 * N + (g // 2) * 3 * N
                here = rows_of((8, 256)) + g * N == high
                for comp in range(3):
                    part = got[start + comp * N : start + comp * N + N]
                    sums[comp] = sums[comp] + jnp.where(here, part, 0.0)
            strength = [jnp.sum(s, axis=0, keepdims=True) for s in sums]
            spots = axis_bits(jnp.broadcast_to(jnp.maximum(ids, 0), (8, 256)))
            points = (spots - jnp.concatenate([base, base], axis=1)).astype(F32)
            row = rows_of(points.shape)
            tile = jnp.where(row < 3, points, 0.0)
            for comp in range(3):
                tile = jnp.where(row == 5 + comp, strength[comp], tile)
            far_out[2 * c] = tile[:, :SLOTS]
            far_out[2 * c + 1] = tile[:, SLOTS:]
            return 0

        lax.fori_loop(0, CELLS, far_gather, 0)
        far = far_out
    else:
        far = far_in

    def far_prep(i, _):
        tile = far[i]
        put(FAR_BASE + i, source_rows(tile, 0.0, 1.0), tile)
        weight[FAR_BASE + i] = moments(
            (tile[0:1], tile[1:2], tile[2:3]), (tile[5:6], tile[6:7], tile[7:8])
        )
        return 0

    lax.fori_loop(0, 2 * CELLS, far_prep, 0)

    for c in range(CELLS):
        used = jnp.int32(0)
        for e in range(NEAR):
            used = used + jnp.where(near_ref[e, c] >= 0, 1, 0)
        count[c] = used

    first_near = base_id - CELLS

    def pair(target, one, two):
        features = jnp.concatenate([feat[one], feat[two]], axis=1)
        features = jnp.concatenate(
            [features, jnp.zeros((SLOTS - FEATS, 2 * SLOTS), BF16)], axis=0
        )
        dist = jnp.maximum(nn(target, features), 0.08)
        root = lax.rsqrt(dist)
        q = root * root * root
        q_high = q.astype(BF16)
        q_low = (q - q_high.astype(F32)).astype(BF16)
        w = jnp.concatenate([weight[one], weight[two]], axis=1)
        return nt(q_high, w) + nt(q_low, w)

    def cell(c, _):
        target = targ[c]
        total = pair(target, FAR_BASE + 2 * c, FAR_BASE + 2 * c + 1)
        used = count[c]

        def step(p, total):
            one = near_ref[2 * p, c] - first_near
            two = jnp.where(2 * p + 1 < used, near_ref[2 * p + 1, c] - first_near, DUMMY)
            return total + pair(target, one, two)

        total = lax.fori_loop(0, (used + 1) // 2, step, total)
        full = jnp.concatenate([total, jnp.zeros((SLOTS, SLOTS - 16), F32)], axis=1).T
        sums = full[0:8] + full[8:16]
        tile, centre = own_tile(CELLS + c)
        at = moved_ref[c] if second else tile
        points = at + centre
        px, py, pz = points[0:1], points[1:2], points[2:3]
        bx, by, bz, ax, ay, az = (sums[r : r + 1] for r in range(6))
        row = rows_of((8, SLOTS))
        vel = jnp.where(
            row == 0, by * pz - bz * py - ax,
            jnp.where(row == 1, bz * px - bx * pz - ay, bx * py - by * px - az),
        )
        vel = jnp.where((row < 3) & (tile[4:5] > 0.0), vel, 0.0)
        if second:
            out_ref[c] = 0.5 * (first_ref[c] + vel)
        else:
            first_ref[c] = vel
            moved_ref[c] = jnp.where(row < 3, tile + 0.25 * vel, 0.0)
        return 0

    lax.fori_loop(0, CELLS, cell, 0)


def run_pass(second, near_list, own_base, ext, *more):
    vmem = pl.BlockSpec(memory_space=pltpu.VMEM)
    smem = pl.BlockSpec(memory_space=pltpu.SMEM)
    tiles = jax.ShapeDtypeStruct((CELLS, 8, SLOTS), F32)
    outs = tiles if second else (tiles, tiles, jax.ShapeDtypeStruct((2 * CELLS, 8, SLOTS), F32))
    return pl.pallas_call(
        functools.partial(pass_kernel, second),
        out_shape=outs,
        in_specs=[smem, smem, vmem] + [vmem] * len(more),
        out_specs=vmem if second else (vmem,) * 3,
        scratch_shapes=[
            pltpu.VMEM((CHUNKS, FEATS, SLOTS), BF16),
            pltpu.VMEM((CHUNKS, 16, SLOTS), BF16),
            pltpu.VMEM((CELLS, SLOTS, SLOTS), BF16),
            pltpu.SMEM((CELLS,), jnp.int32),
            pltpu.VMEM((CELLS, 2 * SLOTS), F32),
        ],
        compiler_params=pltpu.CompilerParams(vmem_limit_bytes=40 * 1024 * 1024),
    )(near_list, own_base, ext, *more)


def route(offsets, strengths, cores, place):
    vmem = pl.BlockSpec(memory_space=pltpu.VMEM)
    sems = [pltpu.SemaphoreType.DMA((N,))] * 4 + [pltpu.SemaphoreType.DMA((2,))] * 2
    sems = sems + [pltpu.SemaphoreType.DMA((N,))] * 8
    return pl.pallas_call(
        route_kernel,
        out_shape=(
            jax.ShapeDtypeStruct((3 * CELLS, 8, SLOTS), F32),
            jax.ShapeDtypeStruct((2, N, 3, N, SLOTS), F32),
        ),
        in_specs=[vmem] * 4,
        out_specs=(vmem, vmem),
        scratch_shapes=[
            pltpu.VMEM((8, offsets.shape[1]), F32),
            pltpu.VMEM((256, 2 * N * SLOTS), BF16),
            pltpu.VMEM((2 * N, 8, SLOTS), F32),
            pltpu.VMEM((N, 2, 8, SLOTS), F32),
            pltpu.VMEM((N, 2, 8, SLOTS), F32),
            pltpu.VMEM((N, 2, 8, SLOTS), F32),
            pltpu.VMEM((8, SLOTS), F32),
            pltpu.VMEM((N, 8, SLOTS), F32),
            pltpu.VMEM((N, 8, SLOTS), F32),
        ] + sems,
        compiler_params=pltpu.CompilerParams(
            collective_id=0, has_side_effects=True, vmem_limit_bytes=40 * 1024 * 1024
        ),
    )(offsets, strengths, cores.reshape(1, -1), place)


def exchange(moved):
    vmem = pl.BlockSpec(memory_space=pltpu.VMEM)
    return pl.pallas_call(
        halo_kernel,
        out_shape=jax.ShapeDtypeStruct((2, CELLS, 8, SLOTS), F32),
        in_specs=[vmem],
        out_specs=vmem,
        scratch_shapes=[pltpu.SemaphoreType.DMA((2,)), pltpu.SemaphoreType.DMA((2,))],
        compiler_params=pltpu.CompilerParams(collective_id=1, has_side_effects=True),
    )(moved)


def per_device(offsets, strengths, cores, place, near_list, far_list):
    device = lax.axis_index("grp") * (N * N) + lax.axis_index("dev")
    own_base = (device * CELLS).astype(jnp.int32).reshape(1)
    ext, table = route(offsets, strengths, cores, place)
    first, moved, far = run_pass(False, near_list, own_base, ext, table, far_list)
    move = exchange(moved)
    out = run_pass(True, near_list, own_base, ext, move, moved, first, far)
    return jnp.transpose(out[:, 0:3], (1, 0, 2)).reshape(3, CELLS * SLOTS)


def solution(mesh):
    row = P(None, ("grp", "dev"))
    return jax.shard_map(
        per_device, mesh=mesh, in_specs=(row, row, P(("grp", "dev")), row, row, row),
        out_specs=row, check_vma=False,
    )
```

time: 402 us -> 133 us (0.33)
  the two profiles are of different devices: /device:TPU:8 before, /device:TPU:1 now
where the time goes in v1:
time: 133 us; the launch traced here: 130 us
  Pallas kernels  127 us (95%)
  local copies, waits for them, and re-layouts  3.63 us (3%)
    pallas_call x2, Pallas kernels, run_pass(): pl.pallas_call(functools.partial(pass_kernel, second), out_shape=outs, in...  69.2 us
    pallas_call x1, Pallas kernels, route(): pl.pallas_call(route_kernel, out_shape=(jax.ShapeDtypeStruct((3 * CELLS,...  48.6 us
    pallas_call x1, Pallas kernels, exchange(): pl.pallas_call(halo_kernel, out_shape=jax.ShapeDtypeStruct((2, CELLS, 8,...  8.81 us
    unnamed x19, local copies, waits for them, and re-layouts  2.99 us

profile of v1, /device:TPU:1, one launch (start us, length us, event | category | flops | bytes accessed | tf_op | source)
XLA Modules:
  0.0 130.3 jit_solution(5569259735321976898)
XLA Ops:
  0.0 0.0 copy-start.8
  0.0 0.7 copy-done.8
  0.7 0.0 copy-start.4
  0.7 0.0 copy-start.5
  0.7 0.0 copy-start.6
  0.7 0.0 copy-start.7
  0.7 0.1 copy.7.rest_1_
  0.8 0.6 copy-done.4
  1.4 0.0 copy-done.5
  1.5 0.0 copy-done.6
  1.5 0.0 copy-done.7
  1.5 0.0 copy-start.3
  1.5 48.6 %shard_map.64 = (f32[48,8,128]{2,1,0:T(8,128)S(1)}, f32[2,8,3,8,128]{4,3,2,1,0:T(8,128)S(1)}) custom-call(f32[3,1024]{1,0:T(4,128)S(1)} %copy-done.4, f32[3,1024]{1,0:T(4,128)S(1)} %copy-done.5, f32[1,1024]{1,0:T(1,128)S(1)} %bitcast.6, s32[2,1024]{1,0:T(2,128)S(1)} %copy-done.6), custom_call_target="tpu_custom_call" | custom-call | tf_op jit(solution)/shard_map/pallas_call | solution.py:482
  50.1 0.0 copy-done.3
  50.1 36.5 %shard_map.65 = (f32[16,8,128]{2,1,0:T(8,128)S(1)}, f32[16,8,128]{2,1,0:T(8,128)S(1)}, f32[32,8,128]{2,1,0:T(8,128)S(1)}) custom-call(s32[14,16]{1,0:T(8,128)S(1)} %copy-done.3, s32[1]{0:T(128)} %bitcast.own_ref, f32[48,8,128]{2,1,0:T(8,128)S(1)} %get-tuple-element.10.ext_ref, f32[2,8,3,8,128]{4,3,2,1,0:T(8,128)S(1)} %get-tuple-element.11.rest_0_, ...), custom_call_target="tpu_custom_call" | custom-call | tf_op jit(solution)/shard_map/pallas_call | solution.py:462
  86.6 0.0 copy-start.1
  86.6 0.6 copy-done.1
  87.2 0.0 copy-start.2
  87.2 8.8 %shard_map.66.rest_0_ = f32[2,16,8,128]{3,2,1,0:T(8,128)} custom-call(f32[16,8,128]{2,1,0:T(8,128)} %copy-done.1), custom_call_target="tpu_custom_call" | custom-call | tf_op jit(solution)/shard_map/pallas_call | solution.py:509
  96.0 0.0 copy-done.2
  96.0 0.0 copy-start
  96.0 0.9 copy-done
  96.9 32.7 %shard_map.67 = f32[16,8,128]{2,1,0:T(8,128)S(1)} custom-call(s32[14,16]{1,0:T(8,128)S(1)} %copy-done.3, s32[1]{0:T(128)} %bitcast.own_ref, f32[48,8,128]{2,1,0:T(8,128)S(1)} %get-tuple-element.10.ext_ref, f32[2,16,8,128]{3,2,1,0:T(8,128)S(1)} %copy-done, f32[16,8,128]{2,1,0:T(8,128)S(1)} %copy-done.2, f32[16,8,128]{2,1,0:T(8,128)S(1)} %get-tuple-element.13.rest_2_, ...), custom_call_target="tpu_custom_call" | custom-call | tf_op jit(solution)/shard_map/pallas_call | solution.py:462
  129.6 0.6 slice_bitcast_fusion
Async XLA Ops:
  0.0 0.7 copy-start.8
  0.7 0.7 copy-start.4
  0.7 0.7 copy-start.5
  0.7 0.7 copy-start.6
  0.7 0.7 copy-start.7
  1.5 48.6 %copy-start.3 = (s32[14,16]{1,0:T(8,128)S(1)}, s32[14,16]{1,0:T(8,128)}, u32[]{:S(2)}) copy-start(s32[14,16]{1,0:T(8,128)} %near_ref.3) | copy-start | bytes 2692
  86.6 0.6 copy-start.1
  87.2 8.8 %copy-start.2 = (f32[16,8,128]{2,1,0:T(8,128)S(1)}, f32[16,8,128]{2,1,0:T(8,128)}, u32[]{:S(2)}) copy-start(f32[16,8,128]{2,1,0:T(8,128)} %copy-done.1) | copy-start | bytes 196612
  96.0 0.9 copy-start

commit v2 on v1

--- a/solution.py
+++ b/solution.py
@@ -24,6 +24,7 @@
 FAR_BASE = NEAR_CHUNKS + 2
 CHUNKS = FAR_BASE + 2 * CELLS
 FEATS = 48
+UNROLL = 8
 
 
 def nt(a, b):
@@ -49,7 +50,7 @@
 
 def route_kernel(
     off_ref, str_ref, core_ref, place_ref, ext_ref, table_ref,
-    fields, spread, send1, recv1, send2, recv2, sums, sums_y, sums_x,
+    fields, spread, send1, recv1, send2, recv2, sums_x, sums_y,
     sx_s, sx_r, sy_s, sy_r, halo_s, halo_r, cy_s, cy_r, cx_s, cx_r, cz_s, cz_r, cc_s, cc_r,
 ):
     dev = lax.axis_index("dev")
@@ -104,6 +105,16 @@
     for t in range(2 * N):
         send1[t] = packed[16 * t : 16 * t + 8] + packed[16 * t + 8 : 16 * t + 16]
 
+    owner_x = owner >> 3
+    shares = jnp.concatenate(
+        [jnp.where(rows_of((8, rows)) == owner_x, both[r : r + 1], 0.0) for r in (5, 6, 7, 13, 14, 15)],
+        axis=0,
+    ).astype(BF16)
+    lane_hot = jnp.where(rows_of((SLOTS, rows)) == (cell_row & (SLOTS - 1)), 1.0, 0.0).astype(BF16)
+    share = nt(shares, lane_hot)
+    for comp in range(3):
+        sums_x[x, comp] = share[8 * comp : 8 * comp + 8] + share[24 + 8 * comp : 32 + 8 * comp]
+
     pl.semaphore_wait(barrier, 3 * (N - 1) + 3)
 
     copies = []
@@ -116,6 +127,15 @@
         )
         copy.start()
         copies.append(copy)
+    x_copies = []
+    for k in range(1, N):
+        copy = pltpu.make_async_remote_copy(
+            src_ref=sums_x.at[x], dst_ref=sums_x.at[x],
+            send_sem=cx_s.at[k], recv_sem=cx_r.at[k],
+            device_id={"dev": x_peer(k) * N + y}, device_id_type=MESH,
+        )
+        copy.start()
+        x_copies.append(copy)
     recv1[x] = send1[pl.ds(2 * x, 2)]
     for copy in copies:
         copy.wait_recv()
@@ -139,11 +159,41 @@
         )
         copy.start()
         copies.append(copy)
+    for copy in x_copies:
+        copy.wait_recv()
+    total = sums_x[0]
+    for k in range(1, N):
+        total = total + sums_x[k]
+    sums_y[y] = total
+    sum_copies = []
+    for k in range(1, N):
+        copy = pltpu.make_async_remote_copy(
+            src_ref=sums_y.at[y], dst_ref=sums_y.at[y],
+            send_sem=cy_s.at[k], recv_sem=cy_r.at[k],
+            device_id={"dev": x * N + y_peer(k)}, device_id_type=MESH,
+        )
+        copy.start()
+        sum_copies.append(copy)
     recv2[y] = send2[y]
+    for copy in sum_copies:
+        copy.wait_recv()
+    total = sums_y[0]
+    for k in range(1, N):
+        total = total + sums_y[k]
+    table_ref[core, z] = total
+    z_copies = []
+    for k in range(1, N):
+        copy = pltpu.make_async_remote_copy(
+            src_ref=table_ref.at[core, z], dst_ref=table_ref.at[core, z],
+            send_sem=cz_s.at[k], recv_sem=cz_r.at[k],
+            device_id={"grp": z_peer(k) * 2 + core}, device_id_type=MESH,
+        )
+        copy.start()
+        z_copies.append(copy)
     for copy in copies[N - 1 :]:
         copy.wait_recv()
 
-    slot_rows, sums_rows, both_all = [], [], []
+    slot_rows = []
     for t in range(2 * N):
         tile = recv2[t // 2, t % 2]
         spot_row = tile[4:5, :] - 1.0
@@ -151,26 +201,11 @@
         slot = (spot_row - cell * SLOTS).astype(jnp.int32)
         cell = cell.astype(jnp.int32)
         two = split2(tile)
-        both_all.append(two.astype(BF16))
         slot_rows.append(jnp.where(rows_of((SLOTS, SLOTS)) == slot, 1.0, 0.0).astype(BF16))
-        sums_rows.append(
-            jnp.where(rows_of((SLOTS, SLOTS)) == cell + y * CELLS, 1.0, 0.0).astype(BF16)
-        )
         for c in range(CELLS):
             spread[16 * c : 16 * c + 16, t * SLOTS : (t + 1) * SLOTS] = jnp.where(
                 cell == c, two, 0.0
             ).astype(BF16)
-    cell_sums = nt(jnp.concatenate(both_all, axis=1), jnp.concatenate(sums_rows, axis=1))
-    sums[...] = cell_sums[0:8] + cell_sums[8:16]
-    sum_copies = []
-    for k in range(1, N):
-        copy = pltpu.make_async_remote_copy(
-            src_ref=sums, dst_ref=sums_y.at[y],
-            send_sem=cy_s.at[k], recv_sem=cy_r.at[k],
-            device_id={"dev": x * N + y_peer(k)}, device_id_type=MESH,
-        )
-        copy.start()
-        sum_copies.append(copy)
     placed = nt(spread[...], jnp.concatenate(slot_rows, axis=1))
     for c in range(CELLS):
         tile = placed[16 * c : 16 * c + 8] + placed[16 * c + 8 : 16 * c + 16]
@@ -187,34 +222,6 @@
         copy.start()
         halo.append(copy)
 
-    total = sums[...]
-    for copy in sum_copies:
-        copy.wait_recv()
-    for k in range(1, N):
-        total = total + sums_y[y_peer(k)]
-    sums_x[x] = total
-    x_copies = []
-    for k in range(1, N):
-        copy = pltpu.make_async_remote_copy(
-            src_ref=sums_x.at[x], dst_ref=sums_x.at[x],
-            send_sem=cx_s.at[k], recv_sem=cx_r.at[k],
-            device_id={"dev": x_peer(k) * N + y}, device_id_type=MESH,
-        )
-        copy.start()
-        x_copies.append(copy)
-    for copy in x_copies:
-        copy.wait_recv()
-    for comp in range(3):
-        table_ref[core, z, comp] = sums_x[:, 5 + comp, :]
-    z_copies = []
-    for k in range(1, N):
-        copy = pltpu.make_async_remote_copy(
-            src_ref=table_ref.at[core, z], dst_ref=table_ref.at[core, z],
-            send_sem=cz_s.at[k], recv_sem=cz_r.at[k],
-            device_id={"grp": z_peer(k) * 2 + core}, device_id_type=MESH,
-        )
-        copy.start()
-        z_copies.append(copy)
     core_copies = []
     for k in range(N):
         if k:
@@ -253,6 +260,15 @@
         copy.wait()
 
 
+def loop(count, at_once, body):
+    def several(i, _):
+        for u in range(at_once):
+            body(i * at_once + u, 0)
+        return 0
+
+    lax.fori_loop(0, count // at_once, several, 0)
+
+
 def axis_bits(ids):
     shifted = ids >> jnp.minimum(rows_of(ids.shape), 2)
     value = shifted & 1
@@ -290,13 +306,13 @@
     second, near_ref, own_ref, ext_ref, *rest
 ):
     if second:
-        move_ref, moved_ref, first_ref, far_in, out_ref, feat, weight, targ, count, acc = rest
+        move_ref, moved_ref, first_ref, far_in, out_ref, feat, weight, targ, far_ids, step_cell, step_one, step_two, acc = rest
     else:
-        table_ref, far_ref, first_ref, moved_ref, far_out, feat, weight, targ, count, acc = rest
+        table_ref, far_ref, first_ref, moved_ref, far_out, feat, weight, targ, far_ids, step_cell, step_one, step_two, acc = rest
     base_id = own_ref[0]
     base = axis_bits(jnp.full((8, SLOTS), base_id, jnp.int32))
 
-    def put(chunk, tile, points):
+    def put(chunk, tile):
         high, mid, low = split3(tile)
         feat[chunk] = jnp.concatenate([high, high, mid, mid, high, low], axis=0).astype(BF16)
 
@@ -319,13 +335,13 @@
         points = at + centre
         core = tile[3:4, :]
         half = 0.5 * core * core
-        put(l, source_rows(points, half, 0.0), points)
+        put(l, source_rows(points, half, 0.0))
         weight[l] = moments(
             (points[0:1], points[1:2], points[2:3]), (tile[5:6], tile[6:7], tile[7:8])
         )
-        return 0
-
-    lax.fori_loop(0, NEAR_CHUNKS, near_prep, 0)
+
+    loop(NEAR_CHUNKS, 8, near_prep)
+    targ[CELLS] = jnp.zeros((SLOTS, FEATS), BF16)
     feat[DUMMY] = jnp.zeros((FEATS, SLOTS), BF16)
     weight[DUMMY] = jnp.zeros((16, SLOTS), BF16)
 
@@ -344,10 +360,9 @@
         high, mid, low = split3(value)
         stack = jnp.concatenate([high, mid, high, mid, low, high], axis=0)
         stack = jnp.concatenate([stack, jnp.zeros((SLOTS - FEATS, SLOTS), F32)], axis=0)
-        targ[c] = stack.T.astype(BF16)
-        return 0
-
-    lax.fori_loop(0, CELLS, target_prep, 0)
+        targ[c] = stack.T[:, :FEATS].astype(BF16)
+
+    loop(CELLS, 4, target_prep)
 
     if not second:
         far_pad = jnp.concatenate(
@@ -355,14 +370,14 @@
         )
         far_pad = jnp.concatenate([far_pad, jnp.full((256 - 192, CELLS), -1.0, F32)], axis=0)
         far_pad = jnp.concatenate([far_pad, jnp.full((256, SLOTS - CELLS), -1.0, F32)], axis=1)
-        acc[...] = jnp.concatenate([far_pad[0:128].T, far_pad[128:256].T], axis=1)[0:CELLS]
+        far_ids[...] = jnp.concatenate([far_pad[0:128].T, far_pad[128:256].T], axis=1)[0:CELLS]
         table = table_ref[...].reshape(2 * N * 3 * N, SLOTS)
         table_high = table.astype(BF16)
         table_low = (table - table_high.astype(F32)).astype(BF16)
         table2 = jnp.concatenate([table_high, table_low], axis=1)
 
         def far_gather(c, _):
-            ids = acc[pl.ds(c, 1), :].astype(jnp.int32)
+            ids = far_ids[pl.ds(c, 1), :].astype(jnp.int32)
             lane_hot = jnp.where(rows_of((SLOTS, 256)) == (ids & 127), 1.0, 0.0).astype(BF16)
             got = nn(table2, jnp.concatenate([lane_hot, lane_hot], axis=0))
             high = ids >> 7
@@ -382,56 +397,70 @@
                 tile = jnp.where(row == 5 + comp, strength[comp], tile)
             far_out[2 * c] = tile[:, :SLOTS]
             far_out[2 * c + 1] = tile[:, SLOTS:]
-            return 0
-
-        lax.fori_loop(0, CELLS, far_gather, 0)
+
+        loop(CELLS, 2, far_gather)
         far = far_out
     else:
         far = far_in
 
     def far_prep(i, _):
         tile = far[i]
-        put(FAR_BASE + i, source_rows(tile, 0.0, 1.0), tile)
+        put(FAR_BASE + i, source_rows(tile, 0.0, 1.0))
         weight[FAR_BASE + i] = moments(
             (tile[0:1], tile[1:2], tile[2:3]), (tile[5:6], tile[6:7], tile[7:8])
         )
-        return 0
-
-    lax.fori_loop(0, 2 * CELLS, far_prep, 0)
-
+
+    loop(2 * CELLS, 8, far_prep)
+
+    first_near = base_id - CELLS
+    total = jnp.int32(CELLS)
     for c in range(CELLS):
-        used = jnp.int32(0)
-        for e in range(NEAR):
-            used = used + jnp.where(near_ref[e, c] >= 0, 1, 0)
-        count[c] = used
-
-    first_near = base_id - CELLS
-
-    def pair(target, one, two):
+        step_cell[c] = c
+        step_one[c] = FAR_BASE + 2 * c
+        step_two[c] = FAR_BASE + 2 * c + 1
+    for c in range(CELLS):
+        for p in range(NEAR // 2):
+            one, two = near_ref[2 * p, c], near_ref[2 * p + 1, c]
+            step_cell[total] = c
+            step_one[total] = one - first_near
+            step_two[total] = jnp.where(two >= 0, two - first_near, DUMMY)
+            total = total + jnp.where(one >= 0, 1, 0)
+    for p in range(UNROLL):
+        step_cell[total + p] = CELLS
+        step_one[total + p] = DUMMY
+        step_two[total + p] = DUMMY
+    acc[...] = jnp.zeros(acc.shape, F32)
+
+    def distances(target, one, two):
         features = jnp.concatenate([feat[one], feat[two]], axis=1)
-        features = jnp.concatenate(
-            [features, jnp.zeros((SLOTS - FEATS, 2 * SLOTS), BF16)], axis=0
-        )
-        dist = jnp.maximum(nn(target, features), 0.08)
-        root = lax.rsqrt(dist)
+        return nn(target, features)
+
+    def powers(dist):
+        root = lax.rsqrt(jnp.maximum(dist, 0.08))
         q = root * root * root
         q_high = q.astype(BF16)
-        q_low = (q - q_high.astype(F32)).astype(BF16)
+        return q_high, (q - q_high.astype(F32)).astype(BF16)
+
+    def sums_of(high, low, one, two):
         w = jnp.concatenate([weight[one], weight[two]], axis=1)
-        return nt(q_high, w) + nt(q_low, w)
+        return nt(high, w) + nt(low, w)
+
+    def steps(i, _):
+        at = [i * UNROLL + u for u in range(UNROLL)]
+        cells = [step_cell[p] for p in at]
+        ones = [step_one[p] for p in at]
+        twos = [step_two[p] for p in at]
+        dists = [distances(targ[cells[u]], ones[u], twos[u]) for u in range(UNROLL)]
+        qs = [powers(d) for d in dists]
+        parts = [sums_of(*qs[u], ones[u], twos[u]) for u in range(UNROLL)]
+        for u in range(UNROLL):
+            acc[cells[u]] += parts[u]
+        return 0
+
+    lax.fori_loop(0, (total + UNROLL - 1) // UNROLL, steps, 0)
 
     def cell(c, _):
-        target = targ[c]
-        total = pair(target, FAR_BASE + 2 * c, FAR_BASE + 2 * c + 1)
-        used = count[c]
-
-        def step(p, total):
-            one = near_ref[2 * p, c] - first_near
-            two = jnp.where(2 * p + 1 < used, near_ref[2 * p + 1, c] - first_near, DUMMY)
-            return total + pair(target, one, two)
-
-        total = lax.fori_loop(0, (used + 1) // 2, step, total)
-        full = jnp.concatenate([total, jnp.zeros((SLOTS, SLOTS - 16), F32)], axis=1).T
+        full = jnp.concatenate([acc[c], jnp.zeros((SLOTS, SLOTS - 16), F32)], axis=1).T
         sums = full[0:8] + full[8:16]
         tile, centre = own_tile(CELLS + c)
         at = moved_ref[c] if second else tile
@@ -449,9 +478,8 @@
         else:
             first_ref[c] = vel
             moved_ref[c] = jnp.where(row < 3, tile + 0.25 * vel, 0.0)
-        return 0
-
-    lax.fori_loop(0, CELLS, cell, 0)
+
+    loop(CELLS, 4, cell)
 
 
 def run_pass(second, near_list, own_base, ext, *more):
@@ -467,9 +495,12 @@
         scratch_shapes=[
             pltpu.VMEM((CHUNKS, FEATS, SLOTS), BF16),
             pltpu.VMEM((CHUNKS, 16, SLOTS), BF16),
-            pltpu.VMEM((CELLS, SLOTS, SLOTS), BF16),
-            pltpu.SMEM((CELLS,), jnp.int32),
+            pltpu.VMEM((CELLS + 1, SLOTS, FEATS), BF16),
             pltpu.VMEM((CELLS, 2 * SLOTS), F32),
+            pltpu.SMEM((CELLS * 8 + UNROLL,), jnp.int32),
+            pltpu.SMEM((CELLS * 8 + UNROLL,), jnp.int32),
+            pltpu.SMEM((CELLS * 8 + UNROLL,), jnp.int32),
+            pltpu.VMEM((CELLS + 1, SLOTS, 16), F32),
         ],
         compiler_params=pltpu.CompilerParams(vmem_limit_bytes=40 * 1024 * 1024),
     )(near_list, own_base, ext, *more)
@@ -494,9 +525,8 @@
             pltpu.VMEM((N, 2, 8, SLOTS), F32),
             pltpu.VMEM((N, 2, 8, SLOTS), F32),
             pltpu.VMEM((N, 2, 8, SLOTS), F32),
-            pltpu.VMEM((8, SLOTS), F32),
-            pltpu.VMEM((N, 8, SLOTS), F32),
-            pltpu.VMEM((N, 8, SLOTS), F32),
+            pltpu.VMEM((N, 3, N, SLOTS), F32),
+            pltpu.VMEM((N, 3, N, SLOTS), F32),
         ] + sems,
         compiler_params=pltpu.CompilerParams(
             collective_id=0, has_side_effects=True, vmem_limit_bytes=40 * 1024 * 1024

time: 133 us -> 80.2 us (0.60); the launches traced: 130 us -> 79.8 us
  Pallas kernels: 127 us -> 76.1 us
    pallas_call x2, Pallas kernels: 69.2 us -> 23.6 us  [run_pass(): pl.pallas_call(functools.partial(pass_kernel, second), out_shape=outs, in...]
    pallas_call x1, Pallas kernels: 48.6 us -> 43.8 us  [route(): pl.pallas_call(route_kernel, out_shape=(jax.ShapeDtypeStruct((3 * CELLS,...]
where the time goes in v2:
time: 80.2 us; the launch traced here: 79.8 us
  Pallas kernels  76.1 us (95%)
  local copies, waits for them, and re-layouts  3.6 us (4%)
    pallas_call x1, Pallas kernels, route(): pl.pallas_call(route_kernel, out_shape=(jax.ShapeDtypeStruct((3 * CELLS,...  43.8 us
    pallas_call x2, Pallas kernels, run_pass(): pl.pallas_call(functools.partial(pass_kernel, second), out_shape=outs, in...  23.6 us
    pallas_call x1, Pallas kernels, exchange(): pl.pallas_call(halo_kernel, out_shape=jax.ShapeDtypeStruct((2, CELLS, 8,...  8.81 us
    unnamed x19, local copies, waits for them, and re-layouts  2.98 us

profile of v2, /device:TPU:1, one launch (start us, length us, event | category | flops | bytes accessed | tf_op | source)
XLA Modules:
  0.0 79.8 jit_solution(2857939961323372907)
XLA Ops:
  0.0 0.0 copy-start.8
  0.0 0.7 copy-done.8
  0.7 0.0 copy-start.4
  0.7 0.0 copy-start.5
  0.7 0.0 copy-start.6
  0.7 0.0 copy-start.7
  0.7 0.1 copy.7.rest_1_
  0.8 0.6 copy-done.4
  1.4 0.0 copy-done.5
  1.5 0.0 copy-done.6
  1.5 0.0 copy-done.7
  1.5 0.0 copy-start.3
  1.5 43.8 %shard_map.64 = (f32[48,8,128]{2,1,0:T(8,128)S(1)}, f32[2,8,3,8,128]{4,3,2,1,0:T(8,128)S(1)}) custom-call(f32[3,1024]{1,0:T(4,128)S(1)} %copy-done.4, f32[3,1024]{1,0:T(4,128)S(1)} %copy-done.5, f32[1,1024]{1,0:T(1,128)S(1)} %bitcast.6, s32[2,1024]{1,0:T(2,128)S(1)} %copy-done.6), custom_call_target="tpu_custom_call" | custom-call | tf_op jit(solution)/shard_map/pallas_call | solution.py:513
  45.2 0.0 copy-done.3
  45.3 13.1 %shard_map.65 = (f32[16,8,128]{2,1,0:T(8,128)S(1)}, f32[16,8,128]{2,1,0:T(8,128)S(1)}, f32[32,8,128]{2,1,0:T(8,128)S(1)}) custom-call(s32[14,16]{1,0:T(8,128)S(1)} %copy-done.3, s32[1]{0:T(128)} %bitcast.own_ref, f32[48,8,128]{2,1,0:T(8,128)S(1)} %get-tuple-element.10.ext_ref, f32[2,8,3,8,128]{4,3,2,1,0:T(8,128)S(1)} %get-tuple-element.11.rest_0_, ...), custom_call_target="tpu_custom_call" | custom-call | tf_op jit(solution)/shard_map/pallas_call | solution.py:490
  58.3 0.0 copy-start.1
  58.3 0.6 copy-done.1
  59.0 0.0 copy-start.2
  59.0 8.8 %shard_map.66.rest_0_ = f32[2,16,8,128]{3,2,1,0:T(8,128)} custom-call(f32[16,8,128]{2,1,0:T(8,128)} %copy-done.1), custom_call_target="tpu_custom_call" | custom-call | tf_op jit(solution)/shard_map/pallas_call | solution.py:539
  67.8 0.0 copy-done.2
  67.8 0.0 copy-start
  67.8 0.9 %copy-done = f32[2,16,8,128]{3,2,1,0:T(8,128)S(1)} copy-done((f32[2,16,8,128]{3,2,1,0:T(8,128)S(1)}, f32[2,16,8,128]{3,2,1,0:T(8,128)}, u32[]{:S(2)}) %copy-start) | copy-done | bytes 131096
  68.7 10.5 %shard_map.67 = f32[16,8,128]{2,1,0:T(8,128)S(1)} custom-call(s32[14,16]{1,0:T(8,128)S(1)} %copy-done.3, s32[1]{0:T(128)} %bitcast.own_ref, f32[48,8,128]{2,1,0:T(8,128)S(1)} %get-tuple-element.10.ext_ref, f32[2,16,8,128]{3,2,1,0:T(8,128)S(1)} %copy-done, f32[16,8,128]{2,1,0:T(8,128)S(1)} %copy-done.2, f32[16,8,128]{2,1,0:T(8,128)S(1)} %get-tuple-element.13.rest_2_, ...), custom_call_target="tpu_custom_call" | custom-call | tf_op jit(solution)/shard_map/pallas_call | solution.py:490
  79.2 0.6 slice_bitcast_fusion
Async XLA Ops:
  0.0 0.7 copy-start.8
  0.7 0.7 copy-start.4
  0.7 0.7 copy-start.5
  0.7 0.7 copy-start.6
  0.7 0.7 copy-start.7
  1.5 43.8 %copy-start.3 = (s32[14,16]{1,0:T(8,128)S(1)}, s32[14,16]{1,0:T(8,128)}, u32[]{:S(2)}) copy-start(s32[14,16]{1,0:T(8,128)} %near_ref.3) | copy-start | bytes 2692
  58.3 0.6 copy-start.1
  59.0 8.8 %copy-start.2 = (f32[16,8,128]{2,1,0:T(8,128)S(1)}, f32[16,8,128]{2,1,0:T(8,128)}, u32[]{:S(2)}) copy-start(f32[16,8,128]{2,1,0:T(8,128)} %copy-done.1) | copy-start | bytes 196612
  67.8 0.9 %copy-start = (f32[2,16,8,128]{3,2,1,0:T(8,128)S(1)}, f32[2,16,8,128]{3,2,1,0:T(8,128)}, u32[]{:S(2)}) copy-start(f32[2,16,8,128]{3,2,1,0:T(8,128)} %shard_map.66.rest_0_) | copy-start | bytes 393220

commit v3 on v2

--- a/solution.py
+++ b/solution.py
@@ -24,7 +24,10 @@
 FAR_BASE = NEAR_CHUNKS + 2
 CHUNKS = FAR_BASE + 2 * CELLS
 FEATS = 48
-UNROLL = 8
+HALF = SLOTS // 2
+LIST = 40
+UNROLL = 12
+FAR_FIRST = (4, 3, 5, 2, 6, 1, 7)
 
 
 def nt(a, b):
@@ -49,9 +52,8 @@
 
 
 def route_kernel(
-    off_ref, str_ref, core_ref, place_ref, ext_ref, table_ref,
-    fields, spread, send1, recv1, send2, recv2, sums_x, sums_y,
-    sx_s, sx_r, sy_s, sy_r, halo_s, halo_r, cy_s, cy_r, cx_s, cx_r, cz_s, cz_r, cc_s, cc_r,
+    rows_ref, ext_ref, table_ref, fields, spread, send1, recv1, send2, recv2,
+    sx_s, sx_r, sy_s, sy_r, cz_s, cz_r, halo_s, halo_r, cc_s, cc_r,
 ):
     dev = lax.axis_index("dev")
     grp = lax.axis_index("grp")
@@ -77,14 +79,12 @@
     pl.semaphore_signal(barrier, 1, device_id={"dev": left}, device_id_type=MESH)
     pl.semaphore_signal(barrier, 1, device_id={"grp": z * 2 + (1 - core)}, device_id_type=MESH)
 
-    rows = off_ref.shape[1]
-    cell_row = place_ref[0:1, :]
-    spot = (cell_row & (CELLS - 1)) * SLOTS + place_ref[1:2, :] + 1
+    rows = rows_ref.shape[1]
+    place = rows_ref[4:5, :].astype(jnp.int32)
+    cell_row = place >> 7
+    spot = (place & (CELLS * SLOTS - 1)) + 1
     owner = (cell_row >> 4) & (N * N - 1)
-    fields[0:3, :] = off_ref[...]
-    fields[3:4, :] = core_ref[...]
-    fields[4:5, :] = spot.astype(F32)
-    fields[5:8, :] = str_ref[...]
+    fields[...] = jnp.where(rows_of((8, rows)) == 4, spot.astype(F32), rows_ref[...])
     both = split2(fields[...])
     earlier = rows_of((SLOTS, 2 * SLOTS)) < lanes_of((SLOTS, 2 * SLOTS))
     counter = jnp.where(earlier | (lanes_of((SLOTS, 2 * SLOTS)) >= SLOTS), 1.0, 0.0).astype(BF16)
@@ -103,7 +103,7 @@
         spread[16 * t : 16 * t + 16, 0:rows] = jnp.where(high == t, both, 0.0).astype(BF16)
     packed = nt(spread[:, 0:rows], low_hot)
     for t in range(2 * N):
-        send1[t] = packed[16 * t : 16 * t + 8] + packed[16 * t + 8 : 16 * t + 16]
+        send1[t // 2, t % 2] = packed[16 * t : 16 * t + 8] + packed[16 * t + 8 : 16 * t + 16]
 
     owner_x = owner >> 3
     shares = jnp.concatenate(
@@ -113,31 +113,24 @@
     lane_hot = jnp.where(rows_of((SLOTS, rows)) == (cell_row & (SLOTS - 1)), 1.0, 0.0).astype(BF16)
     share = nt(shares, lane_hot)
     for comp in range(3):
-        sums_x[x, comp] = share[8 * comp : 8 * comp + 8] + share[24 + 8 * comp : 32 + 8 * comp]
+        part = share[8 * comp : 8 * comp + 8] + share[24 + 8 * comp : 32 + 8 * comp]
+        for t in range(N):
+            send1[t, 2 + comp] = part
 
     pl.semaphore_wait(barrier, 3 * (N - 1) + 3)
 
-    copies = []
-    for k in range(1, N):
+    x_copies = []
+    for k in FAR_FIRST:
         to = x_peer(k)
         copy = pltpu.make_async_remote_copy(
-            src_ref=send1.at[pl.ds(2 * to, 2)], dst_ref=recv1.at[x],
+            src_ref=send1.at[to], dst_ref=recv1.at[x],
             send_sem=sx_s.at[k], recv_sem=sx_r.at[k],
             device_id={"dev": to * N + y}, device_id_type=MESH,
         )
         copy.start()
-        copies.append(copy)
-    x_copies = []
-    for k in range(1, N):
-        copy = pltpu.make_async_remote_copy(
-            src_ref=sums_x.at[x], dst_ref=sums_x.at[x],
-            send_sem=cx_s.at[k], recv_sem=cx_r.at[k],
-            device_id={"dev": x_peer(k) * N + y}, device_id_type=MESH,
-        )
-        copy.start()
         x_copies.append(copy)
-    recv1[x] = send1[pl.ds(2 * x, 2)]
-    for copy in copies:
+    recv1[x] = send1[x]
+    for copy in x_copies:
         copy.wait_recv()
     lane_group = lanes_of((8, SLOTS)) // CAP
     for t in range(N):
@@ -150,7 +143,14 @@
                     part = pltpu.roll(part, turn, 1)
                 tile = part if tile is None else jnp.where(lane_group == g, part, tile)
             send2[t, k] = tile
-    for k in range(1, N):
+    for comp in range(3):
+        total = recv1[0, 2 + comp]
+        for k in range(1, N):
+            total = total + recv1[k, 2 + comp]
+        for t in range(N):
+            send2[t, 2 + comp] = total
+    y_copies = []
+    for k in FAR_FIRST:
         to = y_peer(k)
         copy = pltpu.make_async_remote_copy(
             src_ref=send2.at[to], dst_ref=recv2.at[y],
@@ -158,31 +158,17 @@
             device_id={"dev": x * N + to}, device_id_type=MESH,
         )
         copy.start()
-        copies.append(copy)
-    for copy in x_copies:
+        y_copies.append(copy)
+    recv2[y] = send2[y]
+    for copy in y_copies:
         copy.wait_recv()
-    total = sums_x[0]
-    for k in range(1, N):
-        total = total + sums_x[k]
-    sums_y[y] = total
-    sum_copies = []
-    for k in range(1, N):
-        copy = pltpu.make_async_remote_copy(
-            src_ref=sums_y.at[y], dst_ref=sums_y.at[y],
-            send_sem=cy_s.at[k], recv_sem=cy_r.at[k],
-            device_id={"dev": x * N + y_peer(k)}, device_id_type=MESH,
-        )
-        copy.start()
-        sum_copies.append(copy)
-    recv2[y] = send2[y]
-    for copy in sum_copies:
-        copy.wait_recv()
-    total = sums_y[0]
-    for k in range(1, N):
-        total = total + sums_y[k]
-    table_ref[core, z] = total
+    for comp in range(3):
+        total = recv2[0, 2 + comp]
+        for k in range(1, N):
+            total = total + recv2[k, 2 + comp]
+        table_ref[core, z, comp] = total
     z_copies = []
-    for k in range(1, N):
+    for k in FAR_FIRST:
         copy = pltpu.make_async_remote_copy(
             src_ref=table_ref.at[core, z], dst_ref=table_ref.at[core, z],
             send_sem=cz_s.at[k], recv_sem=cz_r.at[k],
@@ -190,8 +176,6 @@
         )
         copy.start()
         z_copies.append(copy)
-    for copy in copies[N - 1 :]:
-        copy.wait_recv()
 
     slot_rows = []
     for t in range(2 * N):
@@ -222,21 +206,17 @@
         copy.start()
         halo.append(copy)
 
-    core_copies = []
-    for k in range(N):
-        if k:
-            z_copies[k - 1].wait_recv()
-        source = (z + N - k) % N
-        copy = pltpu.make_async_remote_copy(
-            src_ref=table_ref.at[core, source], dst_ref=table_ref.at[core, source],
-            send_sem=cc_s.at[k], recv_sem=cc_r.at[k],
-            device_id={"grp": z * 2 + (1 - core)}, device_id_type=MESH,
-        )
-        copy.start()
-        core_copies.append(copy)
-    for copy in core_copies + halo:
+    for copy in z_copies:
         copy.wait_recv()
-    for copy in copies + sum_copies + x_copies + z_copies + core_copies + halo:
+    core_copy = pltpu.make_async_remote_copy(
+        src_ref=table_ref.at[core], dst_ref=table_ref.at[core],
+        send_sem=cc_s.at[0], recv_sem=cc_r.at[0],
+        device_id={"grp": z * 2 + (1 - core)}, device_id_type=MESH,
+    )
+    core_copy.start()
+    for copy in [core_copy] + halo:
+        copy.wait_recv()
+    for copy in x_copies + y_copies + z_copies + [core_copy] + halo:
         copy.wait_send()
 
 
@@ -299,22 +279,28 @@
     values = (sx, sy, sz, sy * pz - sz * py, sz * px - sx * pz, sx * py - sy * px)
     for r, value in enumerate(values):
         tile = jnp.where(row == r, value, tile)
-    return split2(tile).astype(BF16)
+    return split2(tile)
 
 
 def pass_kernel(
     second, near_ref, own_ref, ext_ref, *rest
 ):
     if second:
-        move_ref, moved_ref, first_ref, far_in, out_ref, feat, weight, targ, far_ids, step_cell, step_one, step_two, acc = rest
+        move_ref, moved_ref, first_ref, far_in, out_ref, feat, weight, targ, far_ids, held, halves, steps_at, acc = rest
     else:
-        table_ref, far_ref, first_ref, moved_ref, far_out, feat, weight, targ, far_ids, step_cell, step_one, step_two, acc = rest
+        table_ref, far_ref, first_ref, moved_ref, far_out, feat, weight, targ, far_ids, held, halves, steps_at, acc = rest
     base_id = own_ref[0]
     base = axis_bits(jnp.full((8, SLOTS), base_id, jnp.int32))
 
     def put(chunk, tile):
         high, mid, low = split3(tile)
-        feat[chunk] = jnp.concatenate([high, high, mid, mid, high, low], axis=0).astype(BF16)
+        stack = jnp.concatenate([high, high, mid, mid, high, low], axis=0)
+        feat[2 * chunk] = stack.astype(BF16)
+        feat[2 * chunk + 1] = pltpu.roll(stack, HALF, 1).astype(BF16)
+
+    def put_weight(chunk, tile):
+        weight[2 * chunk] = tile.astype(BF16)
+        weight[2 * chunk + 1] = pltpu.roll(tile, HALF, 1).astype(BF16)
 
     def own_tile(l):
         tile = ext_ref[l]
@@ -336,14 +322,17 @@
         core = tile[3:4, :]
         half = 0.5 * core * core
         put(l, source_rows(points, half, 0.0))
-        weight[l] = moments(
+        put_weight(l, moments(
             (points[0:1], points[1:2], points[2:3]), (tile[5:6], tile[6:7], tile[7:8])
-        )
-
-    loop(NEAR_CHUNKS, 8, near_prep)
-    targ[CELLS] = jnp.zeros((SLOTS, FEATS), BF16)
-    feat[DUMMY] = jnp.zeros((FEATS, SLOTS), BF16)
-    weight[DUMMY] = jnp.zeros((16, SLOTS), BF16)
+        ))
+        filled = jnp.sum(jnp.where(tile[4:5] > 0.0, 1.0, 0.0)).astype(jnp.int32)
+        held[l] = (filled + HALF - 1) >> 6
+
+    loop(NEAR_CHUNKS, 24, near_prep)
+    targ[2 * CELLS] = jnp.zeros((HALF, FEATS), BF16)
+    for v in range(2):
+        feat[2 * DUMMY + v] = jnp.zeros((FEATS, SLOTS), BF16)
+        weight[2 * DUMMY + v] = jnp.zeros((16, SLOTS), BF16)
 
     def target_prep(c, _):
         tile, centre = own_tile(CELLS + c)
@@ -360,24 +349,22 @@
         high, mid, low = split3(value)
         stack = jnp.concatenate([high, mid, high, mid, low, high], axis=0)
         stack = jnp.concatenate([stack, jnp.zeros((SLOTS - FEATS, SLOTS), F32)], axis=0)
-        targ[c] = stack.T[:, :FEATS].astype(BF16)
-
-    loop(CELLS, 4, target_prep)
+        turned = stack.T[:, :FEATS].astype(BF16)
+        targ[2 * c] = turned[:HALF]
+        targ[2 * c + 1] = turned[HALF:]
+
+    loop(CELLS, 16, target_prep)
 
     if not second:
-        far_pad = jnp.concatenate(
-            [far_ref[...].astype(F32), jnp.full((3, CELLS), -1.0, F32)], axis=0
-        )
-        far_pad = jnp.concatenate([far_pad, jnp.full((256 - 192, CELLS), -1.0, F32)], axis=0)
-        far_pad = jnp.concatenate([far_pad, jnp.full((256, SLOTS - CELLS), -1.0, F32)], axis=1)
-        far_ids[...] = jnp.concatenate([far_pad[0:128].T, far_pad[128:256].T], axis=1)[0:CELLS]
+        far_ids[...] = jnp.full((CELLS, 2 * SLOTS), -1, jnp.int32)
+        far_ids[:, 0:FAR] = far_ref[...]
         table = table_ref[...].reshape(2 * N * 3 * N, SLOTS)
         table_high = table.astype(BF16)
         table_low = (table - table_high.astype(F32)).astype(BF16)
         table2 = jnp.concatenate([table_high, table_low], axis=1)
 
         def far_gather(c, _):
-            ids = far_ids[pl.ds(c, 1), :].astype(jnp.int32)
+            ids = far_ids[pl.ds(c, 1), :]
             lane_hot = jnp.where(rows_of((SLOTS, 256)) == (ids & 127), 1.0, 0.0).astype(BF16)
             got = nn(table2, jnp.concatenate([lane_hot, lane_hot], axis=0))
             high = ids >> 7
@@ -398,7 +385,7 @@
             far_out[2 * c] = tile[:, :SLOTS]
             far_out[2 * c + 1] = tile[:, SLOTS:]
 
-        loop(CELLS, 2, far_gather)
+        loop(CELLS, 4, far_gather)
         far = far_out
     else:
         far = far_in
@@ -406,34 +393,48 @@
     def far_prep(i, _):
         tile = far[i]
         put(FAR_BASE + i, source_rows(tile, 0.0, 1.0))
-        weight[FAR_BASE + i] = moments(
+        put_weight(FAR_BASE + i, moments(
             (tile[0:1], tile[1:2], tile[2:3]), (tile[5:6], tile[6:7], tile[7:8])
-        )
-
-    loop(2 * CELLS, 8, far_prep)
+        ))
+
+    loop(2 * CELLS, 32, far_prep)
 
     first_near = base_id - CELLS
-    total = jnp.int32(CELLS)
-    for c in range(CELLS):
-        step_cell[c] = c
-        step_one[c] = FAR_BASE + 2 * c
-        step_two[c] = FAR_BASE + 2 * c + 1
-    for c in range(CELLS):
-        for p in range(NEAR // 2):
-            one, two = near_ref[2 * p, c], near_ref[2 * p + 1, c]
-            step_cell[total] = c
-            step_one[total] = one - first_near
-            step_two[total] = jnp.where(two >= 0, two - first_near, DUMMY)
-            total = total + jnp.where(one >= 0, 1, 0)
+
+    def listing(c, total):
+        start = c * LIST
+        for i in range(3):
+            halves[start + i] = 2 * FAR_BASE + 4 * c + i
+        n = start + 3
+        for e in range(NEAR):
+            near = near_ref[e, c]
+            at = jnp.where(near >= 0, near - first_near, DUMMY)
+            halves[n] = 2 * at
+            halves[n + 1] = 2 * at + 1
+            n = n + held[at]
+        for i in range(3):
+            halves[n + i] = 2 * DUMMY
+        rounds = (n - start + 3) >> 2
+        size = held[CELLS + c]
+        for h in range(2):
+            for j in range(8):
+                steps_at[total + j] = (start + 4 * j) * 64 + 2 * c + h
+            total = total + jnp.where(size > h, rounds, 0)
+        return total
+
+    held[DUMMY] = 0
+    total = lax.fori_loop(0, CELLS, listing, jnp.int32(0))
+    for i in range(4):
+        halves[CELLS * LIST + i] = 2 * DUMMY
     for p in range(UNROLL):
-        step_cell[total + p] = CELLS
-        step_one[total + p] = DUMMY
-        step_two[total + p] = DUMMY
+        steps_at[total + p] = CELLS * LIST * 64 + 2 * CELLS
     acc[...] = jnp.zeros(acc.shape, F32)
 
-    def distances(target, one, two):
-        features = jnp.concatenate([feat[one], feat[two]], axis=1)
-        return nn(target, features)
+    def joined(ref, rows, four):
+        low = lanes_of((rows, SLOTS)) < HALF
+        return jnp.concatenate(
+            [jnp.where(low, ref[four[i]], ref[four[i + 1] ^ 1]) for i in (0, 2)], axis=1
+        )
 
     def powers(dist):
         root = lax.rsqrt(jnp.maximum(dist, 0.08))
@@ -441,26 +442,26 @@
         q_high = q.astype(BF16)
         return q_high, (q - q_high.astype(F32)).astype(BF16)
 
-    def sums_of(high, low, one, two):
-        w = jnp.concatenate([weight[one], weight[two]], axis=1)
-        return nt(high, w) + nt(low, w)
-
     def steps(i, _):
-        at = [i * UNROLL + u for u in range(UNROLL)]
-        cells = [step_cell[p] for p in at]
-        ones = [step_one[p] for p in at]
-        twos = [step_two[p] for p in at]
-        dists = [distances(targ[cells[u]], ones[u], twos[u]) for u in range(UNROLL)]
+        words = [steps_at[i * UNROLL + u] for u in range(UNROLL)]
+        targets = [word & 63 for word in words]
+        starts = [word >> 6 for word in words]
+        fours = [[halves[p + j] for j in range(4)] for p in starts]
+        dists = [nn(targ[t], joined(feat, FEATS, f)) for t, f in zip(targets, fours)]
         qs = [powers(d) for d in dists]
-        parts = [sums_of(*qs[u], ones[u], twos[u]) for u in range(UNROLL)]
-        for u in range(UNROLL):
-            acc[cells[u]] += parts[u]
+        parts = []
+        for (high, low), f in zip(qs, fours):
+            w = joined(weight, 16, f)
+            parts.append(nt(high, w) + nt(low, w))
+        for t, part in zip(targets, parts):
+            acc[t] += part
         return 0
 
     lax.fori_loop(0, (total + UNROLL - 1) // UNROLL, steps, 0)
 
     def cell(c, _):
-        full = jnp.concatenate([acc[c], jnp.zeros((SLOTS, SLOTS - 16), F32)], axis=1).T
+        full = jnp.concatenate([acc[2 * c], acc[2 * c + 1]], axis=0)
+        full = jnp.concatenate([full, jnp.zeros((SLOTS, SLOTS - 16), F32)], axis=1).T
         sums = full[0:8] + full[8:16]
         tile, centre = own_tile(CELLS + c)
         at = moved_ref[c] if second else tile
@@ -474,64 +475,67 @@
         )
         vel = jnp.where((row < 3) & (tile[4:5] > 0.0), vel, 0.0)
         if second:
-            out_ref[c] = 0.5 * (first_ref[c] + vel)
+            mean = 0.5 * (first_ref[c] + vel)
+            out_ref[:, pl.ds(pl.multiple_of(c * SLOTS, SLOTS), SLOTS)] = mean[0:3]
         else:
             first_ref[c] = vel
             moved_ref[c] = jnp.where(row < 3, tile + 0.25 * vel, 0.0)
 
-    loop(CELLS, 4, cell)
+    loop(CELLS, 16, cell)
 
 
 def run_pass(second, near_list, own_base, ext, *more):
     vmem = pl.BlockSpec(memory_space=pltpu.VMEM)
     smem = pl.BlockSpec(memory_space=pltpu.SMEM)
     tiles = jax.ShapeDtypeStruct((CELLS, 8, SLOTS), F32)
-    outs = tiles if second else (tiles, tiles, jax.ShapeDtypeStruct((2 * CELLS, 8, SLOTS), F32))
+    flat = jax.ShapeDtypeStruct((3, CELLS * SLOTS), F32)
+    outs = flat if second else (tiles, tiles, jax.ShapeDtypeStruct((2 * CELLS, 8, SLOTS), F32))
     return pl.pallas_call(
         functools.partial(pass_kernel, second),
         out_shape=outs,
         in_specs=[smem, smem, vmem] + [vmem] * len(more),
         out_specs=vmem if second else (vmem,) * 3,
         scratch_shapes=[
-            pltpu.VMEM((CHUNKS, FEATS, SLOTS), BF16),
-            pltpu.VMEM((CHUNKS, 16, SLOTS), BF16),
-            pltpu.VMEM((CELLS + 1, SLOTS, FEATS), BF16),
-            pltpu.VMEM((CELLS, 2 * SLOTS), F32),
-            pltpu.SMEM((CELLS * 8 + UNROLL,), jnp.int32),
-            pltpu.SMEM((CELLS * 8 + UNROLL,), jnp.int32),
-            pltpu.SMEM((CELLS * 8 + UNROLL,), jnp.int32),
-            pltpu.VMEM((CELLS + 1, SLOTS, 16), F32),
+            pltpu.VMEM((2 * CHUNKS, FEATS, SLOTS), BF16),
+            pltpu.VMEM((2 * CHUNKS, 16, SLOTS), BF16),
+            pltpu.VMEM((2 * CELLS + 1, HALF, FEATS), BF16),
+            pltpu.VMEM((CELLS, 2 * SLOTS), jnp.int32),
+            pltpu.SMEM((NEAR_CHUNKS + 1,), jnp.int32),
+            pltpu.SMEM((CELLS * LIST + 4,), jnp.int32),
+            pltpu.SMEM((CELLS * 16 + 8 + UNROLL,), jnp.int32),
+            pltpu.VMEM((2 * CELLS + 1, HALF, 16), F32),
         ],
         compiler_params=pltpu.CompilerParams(vmem_limit_bytes=40 * 1024 * 1024),
     )(near_list, own_base, ext, *more)
 
 
 def route(offsets, strengths, cores, place):
+    spots = place[0:1] * SLOTS + place[1:2]
+    tile_rows = jnp.concatenate(
+        [offsets, cores.reshape(1, -1), spots.astype(F32), strengths], axis=0
+    )
     vmem = pl.BlockSpec(memory_space=pltpu.VMEM)
-    sems = [pltpu.SemaphoreType.DMA((N,))] * 4 + [pltpu.SemaphoreType.DMA((2,))] * 2
-    sems = sems + [pltpu.SemaphoreType.DMA((N,))] * 8
+    sems = [pltpu.SemaphoreType.DMA((N,))] * 6 + [pltpu.SemaphoreType.DMA((2,))] * 4
     return pl.pallas_call(
         route_kernel,
         out_shape=(
             jax.ShapeDtypeStruct((3 * CELLS, 8, SLOTS), F32),
             jax.ShapeDtypeStruct((2, N, 3, N, SLOTS), F32),
         ),
-        in_specs=[vmem] * 4,
+        in_specs=[vmem],
         out_specs=(vmem, vmem),
         scratch_shapes=[
             pltpu.VMEM((8, offsets.shape[1]), F32),
             pltpu.VMEM((256, 2 * N * SLOTS), BF16),
-            pltpu.VMEM((2 * N, 8, SLOTS), F32),
-            pltpu.VMEM((N, 2, 8, SLOTS), F32),
-            pltpu.VMEM((N, 2, 8, SLOTS), F32),
-            pltpu.VMEM((N, 2, 8, SLOTS), F32),
-            pltpu.VMEM((N, 3, N, SLOTS), F32),
-            pltpu.VMEM((N, 3, N, SLOTS), F32),
+            pltpu.VMEM((N, 5, 8, SLOTS), F32),
+            pltpu.VMEM((N, 5, 8, SLOTS), F32),
+            pltpu.VMEM((N, 5, 8, SLOTS), F32),
+            pltpu.VMEM((N, 5, 8, SLOTS), F32),
         ] + sems,
         compiler_params=pltpu.CompilerParams(
             collective_id=0, has_side_effects=True, vmem_limit_bytes=40 * 1024 * 1024
         ),
-    )(offsets, strengths, cores.reshape(1, -1), place)
+    )(tile_rows)
 
 
 def exchange(moved):
@@ -542,7 +546,9 @@
         in_specs=[vmem],
         out_specs=vmem,
         scratch_shapes=[pltpu.SemaphoreType.DMA((2,)), pltpu.SemaphoreType.DMA((2,))],
-        compiler_params=pltpu.CompilerParams(collective_id=1, has_side_effects=True),
+        compiler_params=pltpu.CompilerParams(
+            collective_id=1, has_side_effects=True, vmem_limit_bytes=8 * 1024 * 1024
+        ),
     )(moved)
 
 
@@ -550,10 +556,9 @@
     device = lax.axis_index("grp") * (N * N) + lax.axis_index("dev")
     own_base = (device * CELLS).astype(jnp.int32).reshape(1)
     ext, table = route(offsets, strengths, cores, place)
-    first, moved, far = run_pass(False, near_list, own_base, ext, table, far_list)
+    first, moved, far = run_pass(False, near_list, own_base, ext, table, far_list.T)
     move = exchange(moved)
-    out = run_pass(True, near_list, own_base, ext, move, moved, first, far)
-    return jnp.transpose(out[:, 0:3], (1, 0, 2)).reshape(3, CELLS * SLOTS)
+    return run_pass(True, near_list, own_base, ext, move, moved, first, far)
 
 
 def solution(mesh):

time: 80.2 us -> 66.5 us (0.83)
  Pallas kernels: 76.1 us -> 63.9 us
  local copies, waits for them, and re-layouts: 3.6 us -> 0.02 us
  other arithmetic: 0 us -> 1.49 us
    pallas_call x2, Pallas kernels: 23.6 us -> 15.5 us  [run_pass(): pl.pallas_call(functools.partial(pass_kernel, second), out_shape=outs, in...]
    unnamed x19 -> x8, local copies, waits for them, and re-layouts: 2.98 us -> 0.02 us
    pallas_call x1, Pallas kernels: 43.8 us -> 41.2 us  [route(): pl.pallas_call(route_kernel, out_shape=(jax.ShapeDtypeStruct((3 * CELLS,...]
    pallas_call x1, Pallas kernels: 8.81 us -> 7.22 us  [exchange(): pl.pallas_call(halo_kernel, out_shape=jax.ShapeDtypeStruct((2, CELLS, 8,...]
where the time goes in v3:
time: 66.5 us; the launch traced here: 65.5 us
  Pallas kernels  63.9 us (96%)
  other arithmetic  1.49 us (2%)
    pallas_call x1, Pallas kernels, route(): pl.pallas_call(route_kernel, out_shape=(jax.ShapeDtypeStruct((3 * CELLS,...  41.2 us
    pallas_call x2, Pallas kernels, run_pass(): pl.pallas_call(functools.partial(pass_kernel, second), out_shape=outs, in...  15.5 us
    pallas_call x1, Pallas kernels, exchange(): pl.pallas_call(halo_kernel, out_shape=jax.ShapeDtypeStruct((2, CELLS, 8,...  7.22 us

profile of v3, /device:TPU:1, one launch (start us, length us, event | category | flops | bytes accessed | tf_op | source)
XLA Modules:
  0.0 65.5 jit_solution(3871452357365211731)
XLA Ops:
  0.0 0.0 copy-start.2
  0.0 0.0 copy-start.3
  0.0 0.8 %add_convert_fusion = f32[1,1024]{1,0:T(1,128)S(1)} fusion(s32[2,1024]{1,0:T(2,128)} %param.9), kind=kLoop, calls=%fused_computation.1 | loop fusion | flops 3072 | bytes 12288 | tf_op jit(solution)/shard_map/convert_element_type | solution.py:515
  0.8 0.0 copy-done.2
  0.8 0.0 copy-done.3
  0.8 0.7 %pad_maximum_fusion.rows_ref = f32[8,1024]{1,0:T(8,128)S(1)} fusion(f32[3,1024]{1,0:T(4,128)S(1)} %copy-done.2, f32[1,1024]{1,0:T(1,128)S(1)} %add_convert_fusion, f32[1,1024]{1,0:T(1,128)} %bitcast.4, f32[3,1024]{1,0:T(4,128)S(1)} %copy-done.3), kind=kLoop, calls=%fused_computation | loop fusion | flops 24576 | bytes 65536 | tf_op jit(solution)/shard_map/concatenate | solution.py:514
  1.5 0.0 copy-start
  1.5 0.0 copy-start.1
  1.5 41.2 %shard_map.64 = (f32[48,8,128]{2,1,0:T(8,128)S(1)}, f32[2,8,3,8,128]{4,3,2,1,0:T(8,128)S(1)}) custom-call(f32[8,1024]{1,0:T(8,128)S(1)} %pad_maximum_fusion.rows_ref), custom_call_target="tpu_custom_call" | custom-call | tf_op jit(solution)/shard_map/pallas_call | solution.py:519
  42.7 0.0 copy-done
  42.8 0.0 copy-done.1
  42.8 8.3 %shard_map.65 = (f32[16,8,128]{2,1,0:T(8,128)S(1)}, f32[16,8,128]{2,1,0:T(8,128)S(1)}, f32[32,8,128]{2,1,0:T(8,128)S(1)}) custom-call(s32[14,16]{1,0:T(8,128)S(1)} %copy-done, s32[1]{0:T(128)} %bitcast.own_ref, f32[48,8,128]{2,1,0:T(8,128)S(1)} %get-tuple-element.10.ext_ref, f32[2,8,3,8,128]{4,3,2,1,0:T(8,128)S(1)} %get-tuple-element.11.rest_0_, ...), custom_call_target="tpu_custom_call" | custom-call | tf_op jit(solution)/shard_map/pallas_call | solution.py:493
  51.1 7.2 %shard_map.66.rest_0_ = f32[2,16,8,128]{3,2,1,0:T(8,128)S(1)} custom-call(f32[16,8,128]{2,1,0:T(8,128)S(1)} %get-tuple-element.12.moved_ref.rest_1_), custom_call_target="tpu_custom_call" | custom-call | tf_op jit(solution)/shard_map/pallas_call | solution.py:543
  58.3 7.2 %shard_map.67 = f32[3,2048]{1,0:T(4,128)} custom-call(s32[14,16]{1,0:T(8,128)S(1)} %copy-done, s32[1]{0:T(128)} %bitcast.own_ref, f32[48,8,128]{2,1,0:T(8,128)S(1)} %get-tuple-element.10.ext_ref, f32[2,16,8,128]{3,2,1,0:T(8,128)S(1)} %shard_map.66.rest_0_, f32[16,8,128]{2,1,0:T(8,128)S(1)} %get-tuple-element.12.moved_ref.rest_1_, ...), custom_call_target="tpu_custom_call" | custom-call | tf_op jit(solution)/shard_map/pallas_call | solution.py:493
Async XLA Ops:
  0.0 0.8 %copy-start.2 = (f32[3,1024]{1,0:T(4,128)S(1)}, f32[3,1024]{1,0:T(4,128)}, u32[]{:S(2)}) copy-start(f32[3,1024]{1,0:T(4,128)} %param.7) | copy-start | bytes 36868
  0.0 0.8 %copy-start.3 = (f32[3,1024]{1,0:T(4,128)S(1)}, f32[3,1024]{1,0:T(4,128)}, u32[]{:S(2)}) copy-start(f32[3,1024]{1,0:T(4,128)} %param.6) | copy-start | bytes 36868
  1.5 41.2 %copy-start = (s32[14,16]{1,0:T(8,128)S(1)}, s32[14,16]{1,0:T(8,128)}, u32[]{:S(2)}) copy-start(s32[14,16]{1,0:T(8,128)} %near_ref.3) | copy-start | bytes 2692
  1.5 41.2 %copy-start.1 = (s32[189,16]{0,1:T(8,128)S(1)}, s32[189,16]{0,1:T(8,128)}, u32[]{:S(2)}) copy-start(s32[189,16]{0,1:T(8,128)} %param.11) | copy-start | bytes 36292

commit v4 on v3

--- a/solution.py
+++ b/solution.py
@@ -27,6 +27,7 @@
 HALF = SLOTS // 2
 LIST = 40
 UNROLL = 12
+LAST = CELLS * 16 + 8 + UNROLL
 FAR_FIRST = (4, 3, 5, 2, 6, 1, 7)
 
 
@@ -286,9 +287,9 @@
     second, near_ref, own_ref, ext_ref, *rest
 ):
     if second:
-        move_ref, moved_ref, first_ref, far_in, out_ref, feat, weight, targ, far_ids, held, halves, steps_at, acc = rest
+        move_ref, moved_ref, first_ref, far_in, halves, steps_at, out_ref, feat, weight, targ, acc = rest
     else:
-        table_ref, far_ref, first_ref, moved_ref, far_out, feat, weight, targ, far_ids, held, halves, steps_at, acc = rest
+        table_ref, far_ref, first_ref, moved_ref, far_out, halves, steps_at, feat, weight, targ, acc, far_ids, held = rest
     base_id = own_ref[0]
     base = axis_bits(jnp.full((8, SLOTS), base_id, jnp.int32))
 
@@ -325,8 +326,9 @@
         put_weight(l, moments(
             (points[0:1], points[1:2], points[2:3]), (tile[5:6], tile[6:7], tile[7:8])
         ))
-        filled = jnp.sum(jnp.where(tile[4:5] > 0.0, 1.0, 0.0)).astype(jnp.int32)
-        held[l] = (filled + HALF - 1) >> 6
+        if not second:
+            filled = jnp.sum(jnp.where(tile[4:5] > 0.0, 1.0, 0.0)).astype(jnp.int32)
+            held[l] = (filled + HALF - 1) >> 6
 
     loop(NEAR_CHUNKS, 24, near_prep)
     targ[2 * CELLS] = jnp.zeros((HALF, FEATS), BF16)
@@ -422,12 +424,16 @@
             total = total + jnp.where(size > h, rounds, 0)
         return total
 
-    held[DUMMY] = 0
-    total = lax.fori_loop(0, CELLS, listing, jnp.int32(0))
-    for i in range(4):
-        halves[CELLS * LIST + i] = 2 * DUMMY
-    for p in range(UNROLL):
-        steps_at[total + p] = CELLS * LIST * 64 + 2 * CELLS
+    if second:
+        total = steps_at[LAST]
+    else:
+        held[DUMMY] = 0
+        total = lax.fori_loop(0, CELLS, listing, jnp.int32(0))
+        for i in range(4):
+            halves[CELLS * LIST + i] = 2 * DUMMY
+        for p in range(UNROLL):
+            steps_at[total + p] = CELLS * LIST * 64 + 2 * CELLS
+        steps_at[LAST] = total
     acc[...] = jnp.zeros(acc.shape, F32)
 
     def joined(ref, rows, four):
@@ -489,22 +495,27 @@
     smem = pl.BlockSpec(memory_space=pltpu.SMEM)
     tiles = jax.ShapeDtypeStruct((CELLS, 8, SLOTS), F32)
     flat = jax.ShapeDtypeStruct((3, CELLS * SLOTS), F32)
-    outs = flat if second else (tiles, tiles, jax.ShapeDtypeStruct((2 * CELLS, 8, SLOTS), F32))
+    lists = (
+        jax.ShapeDtypeStruct((CELLS * LIST + 4,), jnp.int32),
+        jax.ShapeDtypeStruct((LAST + 1,), jnp.int32),
+    )
+    far = jax.ShapeDtypeStruct((2 * CELLS, 8, SLOTS), F32)
+    outs = flat if second else (tiles, tiles, far) + lists
+    ins = [vmem] * (len(more) - 2) + [smem] * 2 if second else [vmem] * len(more)
+    extra = [] if second else [
+        pltpu.VMEM((CELLS, 2 * SLOTS), jnp.int32), pltpu.SMEM((NEAR_CHUNKS + 1,), jnp.int32)
+    ]
     return pl.pallas_call(
         functools.partial(pass_kernel, second),
         out_shape=outs,
-        in_specs=[smem, smem, vmem] + [vmem] * len(more),
-        out_specs=vmem if second else (vmem,) * 3,
+        in_specs=[smem, smem, vmem] + ins,
+        out_specs=vmem if second else (vmem,) * 3 + (smem,) * 2,
         scratch_shapes=[
             pltpu.VMEM((2 * CHUNKS, FEATS, SLOTS), BF16),
             pltpu.VMEM((2 * CHUNKS, 16, SLOTS), BF16),
             pltpu.VMEM((2 * CELLS + 1, HALF, FEATS), BF16),
-            pltpu.VMEM((CELLS, 2 * SLOTS), jnp.int32),
-            pltpu.SMEM((NEAR_CHUNKS + 1,), jnp.int32),
-            pltpu.SMEM((CELLS * LIST + 4,), jnp.int32),
-            pltpu.SMEM((CELLS * 16 + 8 + UNROLL,), jnp.int32),
             pltpu.VMEM((2 * CELLS + 1, HALF, 16), F32),
-        ],
+        ] + extra,
         compiler_params=pltpu.CompilerParams(vmem_limit_bytes=40 * 1024 * 1024),
     )(near_list, own_base, ext, *more)
 
@@ -556,9 +567,9 @@
     device = lax.axis_index("grp") * (N * N) + lax.axis_index("dev")
     own_base = (device * CELLS).astype(jnp.int32).reshape(1)
     ext, table = route(offsets, strengths, cores, place)
-    first, moved, far = run_pass(False, near_list, own_base, ext, table, far_list.T)
+    first, moved, far, halves, steps_at = run_pass(False, near_list, own_base, ext, table, far_list.T)
     move = exchange(moved)
-    return run_pass(True, near_list, own_base, ext, move, moved, first, far)
+    return run_pass(True, near_list, own_base, ext, move, moved, first, far, halves, steps_at)
 
 
 def solution(mesh):

time: 66.5 us -> 64.8 us (0.974)
  the two profiles are of different devices: /device:TPU:1 before, /device:TPU:4 now
where the time goes in v4:
time: 64.8 us; the launch traced here: 64.5 us
  Pallas kernels  62.9 us (97%)
  other arithmetic  1.49 us (2%)
    pallas_call x1, Pallas kernels, route(): pl.pallas_call(route_kernel, out_shape=(jax.ShapeDtypeStruct((3 * CELLS,...  39.5 us
    pallas_call x2, Pallas kernels, run_pass(): pl.pallas_call(functools.partial(pass_kernel, second), out_shape=outs, in...  16.3 us
    pallas_call x1, Pallas kernels, exchange(): pl.pallas_call(halo_kernel, out_shape=jax.ShapeDtypeStruct((2, CELLS, 8,...  7.16 us

profile of v4, /device:TPU:4, one launch (start us, length us, event | category | flops | bytes accessed | tf_op | source)
XLA Modules:
  0.0 64.5 jit_solution(7624177382311343211)
XLA Ops:
  0.0 0.0 copy-start.2
  0.0 0.0 copy-start.3
  0.0 0.8 %add_convert_fusion = f32[1,1024]{1,0:T(1,128)S(1)} fusion(s32[2,1024]{1,0:T(2,128)} %param.9), kind=kLoop, calls=%fused_computation.1 | loop fusion | flops 3072 | bytes 12288 | tf_op jit(solution)/shard_map/convert_element_type | solution.py:526
  0.8 0.0 copy-done.2
  0.8 0.0 copy-done.3
  0.8 0.7 %pad_maximum_fusion.rows_ref = f32[8,1024]{1,0:T(8,128)S(1)} fusion(f32[3,1024]{1,0:T(4,128)S(1)} %copy-done.2, f32[1,1024]{1,0:T(1,128)S(1)} %add_convert_fusion, f32[1,1024]{1,0:T(1,128)} %bitcast.4, f32[3,1024]{1,0:T(4,128)S(1)} %copy-done.3), kind=kLoop, calls=%fused_computation | loop fusion | flops 24576 | bytes 65536 | tf_op jit(solution)/shard_map/concatenate | solution.py:525
  1.5 0.0 copy-start
  1.5 0.0 copy-start.1
  1.5 39.5 %shard_map.64 = (f32[48,8,128]{2,1,0:T(8,128)S(1)}, f32[2,8,3,8,128]{4,3,2,1,0:T(8,128)S(1)}) custom-call(f32[8,1024]{1,0:T(8,128)S(1)} %pad_maximum_fusion.rows_ref), custom_call_target="tpu_custom_call" | custom-call | tf_op jit(solution)/shard_map/pallas_call | solution.py:530
  41.0 0.0 copy-done
  41.0 0.0 copy-done.1
  41.0 9.7 %shard_map.65 = (f32[16,8,128]{2,1,0:T(8,128)S(1)}, f32[16,8,128]{2,1,0:T(8,128)S(1)}, f32[32,8,128]{2,1,0:T(8,128)S(1)}, s32[644]{0:T(1024)S(1)}, s32[277]{0:T(512)S(1)}) custom-call(s32[14,16]{1,0:T(8,128)S(1)} %copy-done, s32[1]{0:T(128)} %bitcast.own_ref, f32[48,8,128]{2,1,0:T(8,128)S(1)} %get-tuple-element.12.ext_ref, ...), custom_call_target="tpu_custom_call" | custom-call | tf_op jit(solution)/shard_map/pallas_call | solution.py:508
  50.8 7.2 %shard_map.66.rest_0_ = f32[2,16,8,128]{3,2,1,0:T(8,128)S(1)} custom-call(f32[16,8,128]{2,1,0:T(8,128)S(1)} %get-tuple-element.14.moved_ref.rest_1_), custom_call_target="tpu_custom_call" | custom-call | tf_op jit(solution)/shard_map/pallas_call | solution.py:554
  58.0 6.6 %shard_map.67 = f32[3,2048]{1,0:T(4,128)} custom-call(s32[14,16]{1,0:T(8,128)S(1)} %copy-done, s32[1]{0:T(128)} %bitcast.own_ref, f32[48,8,128]{2,1,0:T(8,128)S(1)} %get-tuple-element.12.ext_ref, f32[2,16,8,128]{3,2,1,0:T(8,128)S(1)} %shard_map.66.rest_0_, f32[16,8,128]{2,1,0:T(8,128)S(1)} %get-tuple-element.14.moved_ref.rest_1_, ...), custom_call_target="tpu_custom_call" | custom-call | tf_op jit(solution)/shard_map/pallas_call | solution.py:508
Async XLA Ops:
  0.0 0.8 %copy-start.2 = (f32[3,1024]{1,0:T(4,128)S(1)}, f32[3,1024]{1,0:T(4,128)}, u32[]{:S(2)}) copy-start(f32[3,1024]{1,0:T(4,128)} %param.7) | copy-start | bytes 36868
  0.0 0.8 %copy-start.3 = (f32[3,1024]{1,0:T(4,128)S(1)}, f32[3,1024]{1,0:T(4,128)}, u32[]{:S(2)}) copy-start(f32[3,1024]{1,0:T(4,128)} %param.6) | copy-start | bytes 36868
  1.5 39.5 %copy-start = (s32[14,16]{1,0:T(8,128)S(1)}, s32[14,16]{1,0:T(8,128)}, u32[]{:S(2)}) copy-start(s32[14,16]{1,0:T(8,128)} %near_ref.3) | copy-start | bytes 2692
  1.5 39.5 %copy-start.1 = (s32[189,16]{0,1:T(8,128)S(1)}, s32[189,16]{0,1:T(8,128)}, u32[]{:S(2)}) copy-start(s32[189,16]{0,1:T(8,128)} %param.11) | copy-start | bytes 36292
